TPU v7x, 256 devices: a whole 4x4x8 slice. The times are simulated.
256 devices in a mesh: inst: 64 (over z, x, core), tp: 4 (over y).
Axes of the slice: x: 4, y: 4, z: 8, core: 2. Of those that a mesh axis runs over, the one named last changes fastest.
Arguments:
- queries: bfloat16 [512, 64, 128], P('inst', 'tp'), may hold values from -8 to 8
- keys_cache: bfloat16 [9856, 8, 64, 128], P('inst', 'tp'), may hold values from -12 to 12
- value_block_cache: bfloat16 [9856, 8, 64, 128], P('inst', 'tp'), may hold values from -6 to 6
- block_table: int32 [512, 48], P('inst'), may hold values from -1 to 9855, as said below
- ctx_len: int32 [512], P('inst'), may hold values from 1 to 3072, as said below
- out_weight: bfloat16 [8192, 8192], P('tp', 'inst'), may hold values from -0.25 to 0.25
Outputs:
- mixed: bfloat16 [512, 8192], P('tp', 'inst')
Inputs may be any that keep to these rules, and one draw needn't show every extreme that they name: `block_table`: row n lists the blocks of request n for b < ceil(ctx_len[n] / 64) as j * 154 + page, where j is the instance that holds the block, and -1 after them; no block is listed twice. The blocks of the request of instance h that spans 48 blocks lie on instances j other than h, at page 28 + (((j - h) mod 64) - 1) * 2 + c with 0 <= c < 2; the blocks of its other requests lie on h itself, at pages below 28. `ctx_len`: on each instance one request spans 48 blocks, another exactly 4, and every other one at most 4.
All inputs are finite; a program needn't handle non-finite values.
Results may differ from a plain program's by a relative error of at most 0.0051.
Values may be sent and summed in bfloat16 or wider, within the bound.
A program may use at most 64 MiB of HBM per device.

v0:
```python
import math

import jax
import jax.numpy as jnp
from jax import lax
from jax.sharding import PartitionSpec as P

CAP = 2


very_low = -1e30


def local(queries, keys_cache, value_block_cache, block_table, ctx_len, out_weight):
    inst_count = lax.axis_size("inst")
    home_index = lax.axis_index("inst")
    page_count = keys_cache.shape[0]
    reserved = CAP
    home_pages = page_count - (inst_count - 1) * reserved
    kv_heads = keys_cache.shape[1]
    page_len = keys_cache.shape[2]
    requests, q_heads, head_dim = queries.shape
    query_group_width = q_heads // kv_heads
    slot_count = inst_count * reserved
    max_blocks = block_table.shape[1]
    block_ids = jnp.arange(max_blocks, dtype=jnp.int32)
    valid_tokens = jnp.clip(ctx_len[:, None] - block_ids[None, :] * page_len, 0, page_len)
    live_block = valid_tokens > 0
    lender = block_table // page_count
    local_page = block_table % page_count
    is_home = live_block & (lender == home_index)
    is_lent = live_block & (lender != home_index)
    offset = (lender - home_index) % inst_count
    within = local_page - home_pages - (offset - 1) * reserved
    slot_index = jnp.where(is_lent, lender * reserved + within, slot_count).reshape(-1)
    home_slot = jnp.where(is_home, local_page, home_pages).reshape(-1)
    owner_ids = jnp.broadcast_to(
        jnp.arange(requests, dtype=jnp.int32)[:, None], (requests, max_blocks)
    ).reshape(-1)
    flat_valid = valid_tokens.reshape(-1)
    slot_owner = jnp.zeros((slot_count,), jnp.int32).at[slot_index].set(owner_ids, mode="drop")
    slot_valid = jnp.zeros((slot_count,), jnp.int32).at[slot_index].set(flat_valid, mode="drop")
    home_owner = jnp.zeros((home_pages,), jnp.int32).at[home_slot].set(owner_ids, mode="drop")
    home_valid = jnp.zeros((home_pages,), jnp.int32).at[home_slot].set(flat_valid, mode="drop")
    page_home = (home_index - jnp.arange(inst_count, dtype=jnp.int32)) % inst_count
    lent_home = page_home[1:]
    every_q = lax.all_gather(queries, "inst", axis=0, tiled=True)
    got_owner, got_valid = (
        lax.all_to_all(
            slot_owner.reshape(inst_count, reserved),
            "inst",
            split_axis=0,
            concat_axis=0,
            tiled=True,
        ),
        lax.all_to_all(
            slot_valid.reshape(inst_count, reserved),
            "inst",
            split_axis=0,
            concat_axis=0,
            tiled=True,
        ),
    )
    chosen = (lent_home[:, None] * requests + got_owner[lent_home]).reshape(-1)
    lent_q = every_q[chosen]
    lent_valid = got_valid[lent_home].reshape(-1)
    page_q = jnp.concatenate([queries[home_owner], lent_q], axis=0)
    page_valid = jnp.concatenate([home_valid, lent_valid], axis=0)
    scaling = 1.0 / math.sqrt(head_dim)
    query_groups = page_q.reshape(page_count, kv_heads, query_group_width, head_dim)
    scores = (
        jnp.einsum("pkgd,pktd->pkgt", query_groups, keys_cache, preferred_element_type=jnp.float32)
        * scaling
    )
    token_ids = jnp.arange(page_len, dtype=jnp.int32)
    live_mask = (token_ids[None, :] < page_valid[:, None])[:, None, None, :]
    block_top = jnp.max(jnp.where(live_mask, scores, very_low), axis=-1)
    raised = jnp.where(live_mask, jnp.exp(scores - block_top[..., None]), 0.0)
    block_total = jnp.sum(raised, axis=-1)
    weights = raised.astype(jnp.bfloat16)
    block_out = jnp.einsum(
        "pkgt,pktd->pkgd", weights, value_block_cache, preferred_element_type=jnp.float32
    )
    block_out = block_out.reshape(page_count, q_heads, head_dim)
    block_top = block_top.reshape(page_count, q_heads)
    block_total = block_total.reshape(page_count, q_heads)

    def lent_rows(values):
        lent = values[home_pages:].reshape((inst_count - 1, reserved) + values.shape[1:])
        padded = jnp.concatenate([jnp.zeros((1,) + lent.shape[1:], values.dtype), lent], axis=0)
        return padded[page_home]

    ret_part, ret_top, ret_total = (
        lax.all_to_all(lent_rows(block_out), "inst", split_axis=0, concat_axis=0, tiled=True),
        lax.all_to_all(lent_rows(block_top), "inst", split_axis=0, concat_axis=0, tiled=True),
        lax.all_to_all(lent_rows(block_total), "inst", split_axis=0, concat_axis=0, tiled=True),
    )
    all_part = jnp.concatenate(
        [block_out[:home_pages], ret_part.reshape(slot_count, q_heads, head_dim)], axis=0
    )
    all_top = jnp.concatenate(
        [block_top[:home_pages], ret_top.reshape(slot_count, q_heads)], axis=0
    )
    all_total = jnp.concatenate(
        [block_total[:home_pages], ret_total.reshape(slot_count, q_heads)], axis=0
    )
    all_owner = jnp.concatenate([home_owner, slot_owner], axis=0)
    all_valid = jnp.concatenate([home_valid, slot_valid], axis=0)
    member = (all_owner[None, :] == jnp.arange(requests, dtype=jnp.int32)[:, None]) & (
        all_valid[None, :] > 0
    )
    member = member[:, :, None]
    best_top = jnp.max(jnp.where(member, all_top[None], very_low), axis=1)
    factors = jnp.where(member, jnp.exp(all_top[None] - best_top[:, None, :]), 0.0)
    numerator = jnp.einsum("rsh,shd->rhd", factors, all_part, precision=lax.Precision.HIGHEST)
    denominator = jnp.sum(factors * all_total[None], axis=1)
    attention = (
        (numerator / denominator[..., None])
        .astype(jnp.bfloat16)
        .reshape(requests, q_heads * head_dim)
    )
    terms = jnp.dot(
        lax.all_gather(attention, "inst", axis=0, tiled=True),
        out_weight,
        preferred_element_type=jnp.float32,
    )
    mixed = lax.psum_scatter(terms, "tp", scatter_dimension=0, tiled=True)
    return mixed.astype(jnp.bfloat16)


def solution(mesh):
    return jax.shard_map(
        local,
        mesh=mesh,
        in_specs=(
            P("inst", "tp", None),
            P("inst", "tp", None, None),
            P("inst", "tp", None, None),
            P("inst", None),
            P("inst"),
            P("tp", "inst"),
        ),
        out_specs=P("tp", "inst"),
        check_vma=False,
    )
```

profile of v0, /device:TPU:1, one launch (start us, length us, event | category | flops | bytes accessed | tf_op | source)
XLA Modules:
  0.0 272.0 jit_solution(143186096037829357)
XLA Ops:
  6.5 0.7 all-gather.3.cloned.1.call-update
  7.3 0.8 and_select_fusion
  8.2 2.9 %scatter_custom_fusion.1 = s32[128]{0:T(128)S(1)} fusion(s32[384]{0:T(512)S(1)} %fusion.39, s32[384]{0:T(512)S(1)} %reshape.357, s32[]{:T(128)} %constant.29.clone.1), kind=kCustom, calls=%fused_computation.92 | custom fusion | bytes 516 | tf_op jit(solution)/shard_map/scatter | solution.py:42
  11.1 0.8 all_to_all.25
  11.9 13.0 %all-to-all-start = ((s32[64,1,2]{2,1,0:T(1,128)}), s32[64,1,2]{2,1,0:T(1,128)S(1)}, u32[]{:S(2)}, u32[]{:S(2)}) async-start(s32[64,1,2]{2,1,0:T(1,128)} %bitcast), calls=%async_computation | async-start | bytes 65536 | tf_op jit(solution)/shard_map/all_to_all | solution.py:56
  25.1 2.9 %scatter_custom_fusion.2 = s32[28]{0:T(128)S(1)} fusion(s32[384]{0:T(512)S(1)} %fusion.38, s32[384]{0:T(512)S(1)} %reshape.373, s32[]{:T(128)} %constant.29.clone.1), kind=kCustom, calls=%fused_computation.94 | custom fusion | bytes 116 | tf_op jit(solution)/shard_map/scatter | solution.py:43
  28.2 2.9 %scatter_custom_fusion.3 = s32[128]{0:T(128)S(1)} fusion(s32[384]{0:T(512)S(1)} %fusion.39, s32[384]{0:T(512)S(1)} %reshape.373, s32[]{:T(128)} %constant.29.clone.1), kind=kCustom, calls=%fused_computation.90 | custom fusion | bytes 516 | tf_op jit(solution)/shard_map/scatter | solution.py:41
  31.1 0.7 all_to_all.28
  31.8 2.4 all-to-all-done
  34.2 7.9 %all-to-all-start.1 = ((s32[64,1,2]{2,1,0:T(1,128)}), s32[64,1,2]{2,1,0:T(1,128)S(1)}, u32[]{:S(2)}, u32[]{:S(2)}) async-start(s32[64,1,2]{2,1,0:T(1,128)} %bitcast.2), calls=%async_computation.1 | async-start | bytes 65536 | tf_op jit(solution)/shard_map/all_to_all | solution.py:49
  42.1 2.9 %scatter_custom_fusion = s32[28]{0:T(128)S(1)} fusion(s32[384]{0:T(512)S(1)} %fusion.38, s32[384]{0:T(512)S(1)} %reshape.357, s32[]{:T(128)} %constant.29.clone.1), kind=kCustom, calls=%fused_computation.96 | custom fusion | bytes 116 | tf_op jit(solution)/shard_map/scatter | solution.py:44
  45.0 1.3 gather_fusion.1
  47.1 4.4 %all-to-all-done.1 = s32[64,1,2]{2,1,0:T(1,128)S(1)} async-done(((s32[64,1,2]{2,1,0:T(1,128)}), s32[64,1,2]{2,1,0:T(1,128)S(1)}, u32[]{:S(2)}, u32[]{:S(2)}) %all-to-all-start.1) | async-done | bytes 544 | tf_op jit(solution)/shard_map/all_to_all | solution.py:49
  52.5 39.0 %all-gather.3.cloned.1.call-done = bf16[512,16,128]{2,1,0:T(8,128)(2,1)} async-done(((bf16[8,16,128]{2,1,0:T(8,128)(2,1)}), bf16[512,16,128]{2,1,0:T(8,128)(2,1)}) %all-gather.3.cloned.1.call-update) | async-done | bytes 2097168 | tf_op jit(solution)/shard_map/all_gather | solution.py:47
  91.6 2.3 gather_fusion.3
  93.9 4.8 %select_reduce_fusion = (f32[154,2,8]{2,1,0:T(2,128)S(1)}, f32[154,2,8,64]{3,2,1,0:T(8,128)S(1)}) fusion(pred[154,64]{1,0:T(8,128)(4,1)S(1)} %iota_compare_fusion, bf16[154,2,64,128]{3,2,1,0:T(8,128)(2,1)} %param.7, bf16[126,16,128]{2,1,0:T(8,128)(2,1)S(1)} %gather_fusion.3, bf16[28,16,128]{2,1,0:T(8,128)(2,1)S(1)} %gather_fusion.1), kind=kOutput, calls=%fused_computation.17 | convolution fusion | flops 41156192 | bytes 6327552 | tf_op jit(solution)/shard_map/pkgd,pktd->pkgt/dot_general | solution.py:72
  98.9 1.3 gather_fusion.5
  100.2 6.7 %all-to-all-start.3 = ((f32[64,2,16]{2,1,0:T(2,128)}), f32[64,2,16]{2,1,0:T(2,128)S(1)}, u32[]{:S(2)}, u32[]{:S(2)}) async-start(f32[64,2,16]{2,1,0:T(2,128)} %gather_fusion.5), calls=%async_computation.3 | async-start | bytes 131072 | tf_op jit(solution)/shard_map/all_to_all | solution.py:95
  106.8 1.0 fusion.16
  108.0 1.3 gather_fusion.6
  109.3 7.7 %all-to-all-done.3 = f32[64,2,16]{2,1,0:T(2,128)S(1)} async-done(((f32[64,2,16]{2,1,0:T(2,128)}), f32[64,2,16]{2,1,0:T(2,128)S(1)}, u32[]{:S(2)}, u32[]{:S(2)}) %all-to-all-start.3) | async-done | bytes 8224 | tf_op jit(solution)/shard_map/all_to_all | solution.py:95
  116.9 4.6 %all-to-all-start.4 = ((f32[64,2,16]{2,1,0:T(2,128)}), f32[64,2,16]{2,1,0:T(2,128)S(1)}, u32[]{:S(2)}, u32[]{:S(2)}) async-start(f32[64,2,16]{2,1,0:T(2,128)} %gather_fusion.6), calls=%async_computation.4 | async-start | bytes 131072 | tf_op jit(solution)/shard_map/all_to_all | solution.py:96
  121.6 3.4 %fusion.18 = f32[154,2,8,128]{3,2,1,0:T(8,128)S(1)} fusion(bf16[154,2,64,128]{3,2,1,0:T(8,128)(2,1)} %param.8, f32[154,2,8,64]{3,2,1,0:T(8,128)S(1)} %get-tuple-element.11, f32[154,2,8]{2,1,0:T(2,128)S(1)} %get-tuple-element.10, pred[154,64]{1,0:T(8,128)(4,1)S(1)} %iota_compare_fusion), kind=kOutput, calls=%fused_computation.24 | convolution fusion | flops 40843264 | bytes 6958336 | tf_op jit(solution)/shard_map/pkgt,pktd->pkgd/dot_general | solution.py:81
  125.1 1.6 gather_fusion.4
  126.7 4.9 %all-to-all-done.4 = f32[64,2,16]{2,1,0:T(2,128)S(1)} async-done(((f32[64,2,16]{2,1,0:T(2,128)}), f32[64,2,16]{2,1,0:T(2,128)S(1)}, u32[]{:S(2)}, u32[]{:S(2)}) %all-to-all-start.4) | async-done | bytes 8224 | tf_op jit(solution)/shard_map/all_to_all | solution.py:96
  131.7 5.5 %all-to-all-start.2 = ((f32[64,2,16,128]{3,2,1,0:T(8,128)}), f32[64,2,16,128]{3,2,1,0:T(8,128)S(1)}, u32[]{:S(2)}, u32[]{:S(2)}) async-start(f32[64,2,16,128]{3,2,1,0:T(8,128)} %gather_fusion.4), calls=%async_computation.2 | async-start | bytes 2097152 | tf_op jit(solution)/shard_map/all_to_all | solution.py:94
  138.3 26.9 %all-to-all-done.2 = f32[64,2,16,128]{3,2,1,0:T(8,128)S(1)} async-done(((f32[64,2,16,128]{3,2,1,0:T(8,128)}), f32[64,2,16,128]{3,2,1,0:T(8,128)S(1)}, u32[]{:S(2)}, u32[]{:S(2)}) %all-to-all-start.2) | async-done | bytes 1048608 | tf_op jit(solution)/shard_map/all_to_all | solution.py:94
  165.7 1.9 fusion.13
  167.7 74.8 %all-gather.5.cloned.1.call-done = bf16[512,2048]{1,0:T(8,128)(2,1)} async-done(((bf16[8,2048]{1,0:T(8,128)(2,1)}), bf16[512,2048]{1,0:T(8,128)(2,1)}) %all-gather.5.cloned.1.call-update) | async-done | bytes 2097168 | tf_op jit(solution)/shard_map/all_gather | solution.py:123
  242.5 3.0 %fusion.56 = f32[512,128]{1,0:T(8,128)} fusion(bf16[512,2048]{1,0:T(8,128)(2,1)} %all-gather.5.cloned.1.call-done, bf16[2048,128]{1,0:T(8,128)(2,1)S(1)} %copy-done), kind=kOutput, calls=%fused_computation.102 | convolution fusion | flops 268435456 | bytes 2883584 | tf_op jit(solution)/shard_map/dot_general | solution.py:122
  245.6 18.4 %reduce-scatter.2.cloned.1.call-done = f32[128,128]{1,0:T(8,128)} async-done(((f32[512,128]{1,0:T(8,128)}), f32[128,128]{1,0:T(8,128)}) %reduce-scatter.2.cloned.1.call-update) | async-done | bytes 65552 | tf_op jit(solution)/shard_map/reduce_scatter | solution.py:127
  264.0 1.5 convert_element_type.11
  (55 shorter events, 4.4 us)
Async XLA Ops:
  6.5 236.0 %copy-start = (bf16[2048,128]{1,0:T(8,128)(2,1)S(1)}, bf16[2048,128]{1,0:T(8,128)(2,1)}, u32[]{:S(2)}) copy-start(bf16[2048,128]{1,0:T(8,128)(2,1)} %param.11) | copy-start | bytes 1572868
  6.5 85.0 %all-gather.3.cloned.1.call-start = ((), (), s32[]{:S(2)}) async-start(), calls=%async_computation.6 | async-start | bytes 2129920 | tf_op jit(solution)/shard_map/all_gather | solution.py:47
  11.9 22.3 %all-to-all-start = ((s32[64,1,2]{2,1,0:T(1,128)}), s32[64,1,2]{2,1,0:T(1,128)S(1)}, u32[]{:S(2)}, u32[]{:S(2)}) async-start(s32[64,1,2]{2,1,0:T(1,128)} %bitcast), calls=%async_computation | async-start | bytes 65536 | tf_op jit(solution)/shard_map/all_to_all | solution.py:56
  34.2 17.3 %all-to-all-start.1 = ((s32[64,1,2]{2,1,0:T(1,128)}), s32[64,1,2]{2,1,0:T(1,128)S(1)}, u32[]{:S(2)}, u32[]{:S(2)}) async-start(s32[64,1,2]{2,1,0:T(1,128)} %bitcast.2), calls=%async_computation.1 | async-start | bytes 65536 | tf_op jit(solution)/shard_map/all_to_all | solution.py:49
  100.2 16.8 %all-to-all-start.3 = ((f32[64,2,16]{2,1,0:T(2,128)}), f32[64,2,16]{2,1,0:T(2,128)S(1)}, u32[]{:S(2)}, u32[]{:S(2)}) async-start(f32[64,2,16]{2,1,0:T(2,128)} %gather_fusion.5), calls=%async_computation.3 | async-start | bytes 131072 | tf_op jit(solution)/shard_map/all_to_all | solution.py:95
  116.9 14.8 %all-to-all-start.4 = ((f32[64,2,16]{2,1,0:T(2,128)}), f32[64,2,16]{2,1,0:T(2,128)S(1)}, u32[]{:S(2)}, u32[]{:S(2)}) async-start(f32[64,2,16]{2,1,0:T(2,128)} %gather_fusion.6), calls=%async_computation.4 | async-start | bytes 131072 | tf_op jit(solution)/shard_map/all_to_all | solution.py:96
  131.7 33.5 %all-to-all-start.2 = ((f32[64,2,16,128]{3,2,1,0:T(8,128)}), f32[64,2,16,128]{3,2,1,0:T(8,128)S(1)}, u32[]{:S(2)}, u32[]{:S(2)}) async-start(f32[64,2,16,128]{3,2,1,0:T(8,128)} %gather_fusion.4), calls=%async_computation.2 | async-start | bytes 2097152 | tf_op jit(solution)/shard_map/all_to_all | solution.py:94
  137.2 105.3 %all-gather.5.cloned.1.call-start = ((), (), s32[]{:S(2)}) async-start(), calls=%async_computation.7 | async-start | bytes 2129920 | tf_op jit(solution)/shard_map/all_gather | solution.py:123
  167.7 96.3 %reduce-scatter.2.cloned.1.call-start = ((), (), s32[]{:S(2)}) async-start(), calls=%async_computation.8 | async-start | bytes 327680 | tf_op jit(solution)/shard_map/reduce_scatter | solution.py:127
Sparse Core Ops, SparseCore 0:
  10.1 81.3 all-gather.2
  167.8 74.6 all-gather.4
  245.7 18.2 reduce-scatter.1
where the time goes:
time: 274 us; the launch traced here: 272 us
  waiting for transfers between devices  179 us (65%)
  starting transfers between devices  37.8 us (14%)
  local copies, waits for them, and re-layouts  24.2 us (9%)
  between operations  13.4 us (5%)
  matrix products  13.2 us (5%)
  other arithmetic  4.21 us (2%)
    all_gather x1, waiting for transfers between devices, local(): lax.all_gather(attention, 'inst', axis=0, tiled=True)  74.8 us
    all_gather x1, waiting for transfers between devices, local(): every_q = lax.all_gather(queries, 'inst', axis=0, tiled=True)  39 us
    all_to_all x1, waiting for transfers between devices, local(): lax.all_to_all(lent_rows(block_out), 'inst', split_axis=0, concat_axis=0,...  26.9 us
    reduce_scatter x1, waiting for transfers between devices, local(): mixed = lax.psum_scatter(terms, 'tp', scatter_dimension=0, tiled=True)  18.4 us
    all_to_all x1, starting transfers between devices, local(): lax.all_to_all(slot_valid.reshape(inst_count, reserved), 'inst', split_ax...  13 us
    all_to_all x1, starting transfers between devices, local(): lax.all_to_all(slot_owner.reshape(inst_count, reserved), 'inst', split_ax...  7.91 us
    all_to_all x1, waiting for transfers between devices, local(): lax.all_to_all(lent_rows(block_top), 'inst', split_axis=0, concat_axis=0,...  7.66 us
    all_to_all x1, starting transfers between devices, local(): lax.all_to_all(lent_rows(block_top), 'inst', split_axis=0, concat_axis=0,...  6.68 us
  transfers between devices with their start and end apart: 8, of which 8 were waited for; matrix products, arithmetic and copies ran while one was open for 9% of the time, Pallas kernels for 0%

commit v1 on v0

v1 whole, which is shorter than its diff:
```python
import math

import jax
import jax.numpy as jnp
from jax import lax
from jax.experimental import pallas as pl
from jax.experimental.pallas import tpu as pltpu
from jax.sharding import PartitionSpec as P

MESH = pl.DeviceIdType.MESH
F32 = jnp.float32
BF16 = jnp.bfloat16

N_INST = 64
TP = 4
ZN, XN = 8, 4
R = 8
HEADS = 16
KV = 2
GROUP = HEADS // KV
HD = 128
BT = 64
CAP = 2
PAGES = 154
HOME = PAGES - CAP * (N_INST - 1)
OTHERB = 4
MAXB = 48
LOW = -1e30
SCALE = math.log2(math.e) / math.sqrt(HD)
NEAR = (1, 7, 2, 6, 3, 5, 4)


def iota(shape, dim):
    return lax.broadcasted_iota(jnp.int32, shape, dim)


def dot(a, b):
    return jnp.dot(a, b, preferred_element_type=F32)


def dot_t(a, b):
    return lax.dot_general(a, b, (((1,), (1,)), ((), ())), preferred_element_type=F32)


def remote(src, dst, send, recv, where):
    return pltpu.make_async_remote_copy(
        src_ref=src, dst_ref=dst, send_sem=send, recv_sem=recv, device_id=where, device_id_type=MESH
    )


def drain(ref, sem):
    pltpu.make_async_copy(ref, ref, sem).wait()


def kernel(
    q_ref, k_hbm, v_hbm, tab_ref, ctx_ref, w_hbm, out_ref,
    kbuf, vbuf, wbuf, qall, meta, abuf, rsend, rrecv, a2, a2f, tsh, own, ysend, yrecv,
    ld, qs, qr, ms, mr, zs, zr, xs, xr, cs, cr, rs, rr, gs, gr, ys, yr,
):
    me = lax.axis_index("inst")
    tp = lax.axis_index("tp")
    z, xc = me // 8, me % 8
    x, c = xc // 2, xc % 2

    barrier = pltpu.get_barrier_semaphore()

    def greet(d, carry):
        pl.semaphore_signal(barrier, inc=1, device_id={"inst": (me + d) % N_INST}, device_id_type=MESH)
        return carry

    lax.fori_loop(1, N_INST, greet, 0)
    for d in range(1, TP):
        pl.semaphore_signal(barrier, inc=1, device_id={"tp": (tp + d) % TP}, device_id_type=MESH)

    half = HEADS * HD // 2
    loads = [
        pltpu.make_async_copy(k_hbm.at[pl.ds(0, HOME)], kbuf.at[pl.ds(0, HOME)], ld.at[0]),
        pltpu.make_async_copy(v_hbm.at[pl.ds(0, HOME)], vbuf.at[pl.ds(0, HOME)], ld.at[1]),
        pltpu.make_async_copy(k_hbm.at[pl.ds(HOME, PAGES - HOME)], kbuf.at[pl.ds(HOME, PAGES - HOME)], ld.at[2]),
        pltpu.make_async_copy(v_hbm.at[pl.ds(HOME, PAGES - HOME)], vbuf.at[pl.ds(HOME, PAGES - HOME)], ld.at[3]),
        pltpu.make_async_copy(w_hbm.at[pl.ds(0, half)], wbuf.at[0], ld.at[4]),
        pltpu.make_async_copy(w_hbm.at[pl.ds(half, half)], wbuf.at[1], ld.at[5]),
    ]
    for copy in loads:
        copy.start()

    tab = tab_ref[...]
    row8, lane8 = iota((R, 128), 0), iota((R, 128), 1)
    ctx = jnp.zeros((R, 1), jnp.int32)
    for n in range(R):
        ctx = jnp.where(iota((R, 1), 0) == n, ctx_ref[n], ctx)
    lender, slot = lane8 >> 1, lane8 & 1
    target = lender * PAGES + HOME + (((lender - me) & (N_INST - 1)) - 1) * CAP + slot
    target = jnp.where(lender == me, -5, target)
    slots = jnp.zeros((R, 128), jnp.int32)
    home = jnp.zeros((R, 128), jnp.int32)
    for b in range(MAXB):
        valid = jnp.clip(ctx - b * BT, 0, BT)
        page = tab[:, b : b + 1]
        slots = slots + jnp.where(page == target, valid, 0)
        if b < OTHERB:
            home = home + jnp.where(page == me * PAGES + lane8, valid, 0)
    longest = jnp.sum(jnp.where(ctx > OTHERB * BT, iota((R, 1), 0), 0).astype(F32), axis=0, keepdims=True)
    slots = jnp.sum(slots.astype(F32), axis=0, keepdims=True)
    slots = jnp.where(lane8[0:1] == 2 * me, longest, slots)
    meta[me] = slots.astype(jnp.int32)
    q = q_ref[...]
    pick = iota((HEADS, 128), 1).astype(F32) == longest * HEADS + iota((HEADS, 128), 0).astype(F32)
    qall[me] = dot(pick.astype(F32).astype(BF16), q).astype(BF16)

    pl.semaphore_wait(barrier, N_INST - 1 + TP - 1)

    def send_q(dest, dz):
        remote(qall.at[me], qall.at[me], qs, qr.at[dz], {"inst": dest}).start()
        remote(meta.at[me], meta.at[me], ms, mr.at[dz], {"inst": dest}).start()

    def near(i):
        step = (i + 1) // 2
        return (step * (1 - 2 * ((i + 1) % 2))) & (ZN - 1)

    for e in range(1, 8):
        send_q(z * 8 + ((xc + e) & 7), 0)

    def send_qs(i, carry):
        dz = near(i)
        for e in range(8):
            send_q(((z + dz) & 7) * 8 + e, dz)
        return carry

    lax.fori_loop(1, ZN, send_qs, 0)

    prow, plane = iota((128, 128), 0), iota((128, 128), 1)
    perm = plane == (prow & 7) * HEADS + (prow >> 6) * GROUP + ((prow >> 3) & 7)
    qp = dot(perm.astype(F32).astype(BF16), q).astype(BF16)
    tokens = HOME * BT
    spread = (iota((128, tokens), 1) >> 6) == iota((128, tokens), 0)
    vtok = dot(home.astype(F32).astype(BF16), spread.astype(F32).astype(BF16))
    bias = jnp.where((iota((R, tokens), 1) & (BT - 1)).astype(F32) < vtok, 0.0, LOW)
    loads[0].wait()
    loads[1].wait()
    short = iota((R, 1), 0).astype(F32) != longest
    outs = []
    for k in range(KV):
        keys = kbuf[pl.ds(0, HOME), k].reshape(tokens, HD)
        values = vbuf[pl.ds(0, HOME), k].reshape(tokens, HD)
        s = dot_t(qp[k * 64 : (k + 1) * 64], keys).reshape(GROUP, R, tokens) * SCALE + bias[None]
        top = jnp.max(s, axis=-1, keepdims=True)
        p = jnp.exp2(s - top)
        total = jnp.sum(p, axis=-1, keepdims=True)
        o = dot(p.reshape(64, tokens).astype(BF16), values).reshape(GROUP, R, HD)
        outs.append(jnp.where(short[None], o / total, 0.0))
    for g in range(GROUP):
        abuf[me, :, g * HD : (g + 1) * HD] = jnp.concatenate([outs[0][g], outs[1][g]], axis=0).astype(BF16)

    zc = {}
    for d in NEAR:
        zc[d] = remote(abuf.at[me], abuf.at[me], zs.at[d], zr.at[d], {"inst": ((z + d) & 7) * 8 + xc})
        zc[d].start()

    kv_of = (iota((HEADS, 256), 1) >> 6) & 1
    kv_bias = jnp.where(kv_of == iota((HEADS, 256), 0) // GROUP, 0.0, LOW)
    lane256 = iota((8, 256), 1)
    lane16 = iota((HEADS, 128), 1)
    loads[2].wait()
    loads[3].wait()

    def lend(zh):
        rows = meta[pl.ds(zh * 8, 8)].reshape(8, 128)
        v = [jnp.sum(jnp.where(lane8 == 2 * me + s, rows, 0).astype(F32), axis=-1, keepdims=True) for s in range(CAP)]
        limit = jnp.where(lane256 < 128, v[0], v[1])
        bias8 = jnp.where((lane256 & (BT - 1)).astype(F32) < limit, 0.0, LOW)
        pages = [HOME - CAP + CAP * ((me - (zh * 8 + i)) & (N_INST - 1)) for i in range(8)]
        ss = [
            dot_t(qall[zh * 8 + i], kbuf[pl.ds(pages[i], CAP)].reshape(256, HD)) * SCALE
            + (bias8[i : i + 1] + kv_bias)
            for i in range(8)
        ]
        for i in range(8):
            top = jnp.maximum(jnp.max(ss[i], axis=-1, keepdims=True), -1e20).astype(BF16).astype(F32)
            p = jnp.exp2(ss[i] - top)
            total = jnp.sum(p, axis=-1, keepdims=True)
            o = dot(p.astype(BF16), vbuf[pl.ds(pages[i], CAP)].reshape(256, HD))
            high = total.astype(BF16).astype(F32)
            stats = jnp.where(lane16 < 64, top, jnp.where(lane16 < 96, high, total - high))
            rsend[zh * 8 + i, 0:16] = o.astype(BF16)
            rsend[zh * 8 + i, 16:32] = stats.astype(BF16)

    def send_r(h):
        remote(rsend.at[h], rrecv.at[me], rs, rr, {"inst": h}).start()

    drain(qall.at[pl.ds(0, 7)], qr.at[0])
    drain(meta.at[pl.ds(0, 7)], mr.at[0])
    lend(z)
    for e in range(1, 8):
        send_r(z * 8 + ((xc + e) & 7))

    def lend_z(i, carry):
        dz = near(i)
        drain(qall.at[pl.ds(0, 8)], qr.at[dz])
        drain(meta.at[pl.ds(0, 8)], mr.at[dz])
        zh = (z - dz) & 7
        lend(zh)
        for e in range(8):
            send_r(zh * 8 + e)
        return carry

    lax.fori_loop(1, ZN, lend_z, 0)

    xcopies = []

    def along_x(zz, k):
        for d in range(1, XN):
            block = abuf.at[zz * 8 + xc]
            copy = remote(block, block, xs.at[4 * k + d], xr.at[4 * k + d], {"inst": z * 8 + ((x + d) & 3) * 2 + c})
            copy.start()
            xcopies.append((d, copy))

    along_x(z, 0)
    for d in NEAR:
        zc[d].wait_recv()
        along_x((z - d) & 7, d)

    rrecv[me, 0:16] = jnp.zeros((HEADS, HD), BF16)
    rrecv[me, 16:32] = jnp.where(lane16 < 64, -1e20, 0.0).astype(BF16)
    drain(rrecv.at[pl.ds(0, N_INST - 1)], rr)

    def tops(i, best):
        for e in range(8):
            best = jnp.maximum(best, rrecv[i * 8 + e, 16:32].astype(F32))
        return best

    best = lax.fori_loop(0, 8, tops, jnp.full((HEADS, HD), -1e20, F32))
    best = jnp.broadcast_to(best[:, 0:1], (HEADS, HD))

    def merge(i, carry):
        num, den = carry
        for e in range(8):
            stats = rrecv[i * 8 + e, 16:32].astype(F32)
            f = jnp.exp2(jnp.broadcast_to(stats[:, 0:1], (HEADS, HD)) - best)
            num = num + f * rrecv[i * 8 + e, 0:16].astype(F32)
            den = den + f * stats
        return num, den

    zero = jnp.zeros((HEADS, HD), F32)
    num, den = lax.fori_loop(0, 8, merge, (zero, zero))
    a2[me] = (num / (den[:, 64:65] + den[:, 96:97])).astype(BF16)

    def send_a2(d, carry):
        remote(a2.at[me], a2.at[me], gs, gr, {"inst": (me + d) % N_INST}).start()
        return carry

    lax.fori_loop(1, N_INST, send_a2, 0)

    sib = {"inst": me + 1 - 2 * c}
    ccopies = []

    def across(xx, k):
        for zz in range(ZN):
            block = abuf.at[zz * 8 + xx * 2 + c]
            copy = remote(block, block, cs.at[zz * 4 + k], cr.at[zz * 4 + k], sib)
            copy.start()
            ccopies.append(copy)

    across(x, 0)
    for dd in (1, 3, 2):
        for d, copy in xcopies:
            if d == dd:
                copy.wait_recv()
        across((x - dd) & 3, dd)
    for copy in ccopies:
        copy.wait_recv()

    loads[4].wait()
    loads[5].wait()

    def project(i, carry):
        a = abuf[pl.ds(i * 16, 16)].reshape(256, half)
        t0 = dot(a, wbuf[0]).reshape(16, 16, HD)
        t1 = dot(a, wbuf[1]).reshape(16, 16, HD)
        tsh[pl.ds(i * 16, 16)] = t0[:, 0:8] + t1[:, 8:16]
        return carry

    lax.fori_loop(0, 4, project, 0)

    owners = meta[...].reshape(N_INST, 128)
    mine = iota((N_INST, 128), 1) == 2 * iota((N_INST, 128), 0)
    own[...] = jnp.broadcast_to(
        jnp.sum(jnp.where(mine, owners, 0).astype(F32), axis=-1, keepdims=True), (N_INST, 128)
    )
    drain(a2.at[pl.ds(0, N_INST - 1)], gr)
    a2f[...] = a2[...].astype(F32).reshape(N_INST * HEADS, HD)
    left = [a2f[pl.ds(h, N_INST, stride=HEADS), :].astype(BF16) for h in range(HEADS)]
    t2 = dot(jnp.concatenate(left[:8], axis=1), wbuf[0]) + dot(jnp.concatenate(left[8:], axis=1), wbuf[1])
    frow = row8.astype(F32)
    for i in range(N_INST):
        t = tsh[i] + jnp.where(frow == own[i : i + 1, :], t2[i : i + 1, :], 0.0)
        ysend[i // 16, (i % 16) * 8 : (i % 16) * 8 + 8, :] = t
    ycopies = []
    for d in range(1, TP):
        to = (tp + d) % TP
        copy = remote(ysend.at[to], yrecv.at[d], ys.at[d], yr.at[d], {"tp": to})
        copy.start()
        ycopies.append(copy)
    for copy in ycopies:
        copy.wait_recv()
    out_ref[...] = (ysend[tp] + yrecv[1] + yrecv[2] + yrecv[3]).astype(BF16)

    for copy in ycopies + ccopies + [copy for _, copy in xcopies] + list(zc.values()):
        copy.wait_send()
    drain(qall.at[pl.ds(0, N_INST - 1)], qs)
    drain(meta.at[pl.ds(0, N_INST - 1)], ms)
    drain(rsend.at[pl.ds(0, N_INST - 1)], rs)
    drain(a2.at[pl.ds(0, N_INST - 1)], gs)


def local(queries, keys_cache, value_block_cache, block_table, ctx_len, out_weight):
    dma = pltpu.SemaphoreType.DMA
    vmem = pl.BlockSpec(memory_space=pltpu.VMEM)
    hbm = pl.BlockSpec(memory_space=pl.ANY)
    smem = pl.BlockSpec(memory_space=pltpu.SMEM)
    return pl.pallas_call(
        kernel,
        out_shape=jax.ShapeDtypeStruct((N_INST * R // TP, HD), BF16),
        in_specs=[vmem, hbm, hbm, vmem, smem, hbm],
        out_specs=vmem,
        scratch_shapes=[
            pltpu.VMEM((PAGES, KV, BT, HD), BF16),
            pltpu.VMEM((PAGES, KV, BT, HD), BF16),
            pltpu.VMEM((2, HEADS * HD // 2, HD), BF16),
            pltpu.VMEM((N_INST, HEADS, HD), BF16),
            pltpu.VMEM((N_INST, 1, 128), jnp.int32),
            pltpu.VMEM((N_INST, HEADS, GROUP * HD), BF16),
            pltpu.VMEM((N_INST, 32, HD), BF16),
            pltpu.VMEM((N_INST, 32, HD), BF16),
            pltpu.VMEM((N_INST, HEADS, HD), BF16),
            pltpu.VMEM((N_INST * HEADS, HD), F32),
            pltpu.VMEM((N_INST, R, HD), F32),
            pltpu.VMEM((N_INST, 128), F32),
            pltpu.VMEM((TP, N_INST * R // TP, HD), F32),
            pltpu.VMEM((TP, N_INST * R // TP, HD), F32),
            dma((6,)),
            dma, dma((ZN,)), dma, dma((ZN,)),
            dma((ZN,)), dma((ZN,)),
            dma((4 * ZN,)), dma((4 * ZN,)),
            dma((4 * ZN,)), dma((4 * ZN,)),
            dma, dma,
            dma, dma,
            dma((TP,)), dma((TP,)),
        ],
        name="paged_decode",
        compiler_params=pltpu.CompilerParams(
            collective_id=0, has_side_effects=True, vmem_limit_bytes=48 * 2**20
        ),
    )(
        queries.reshape(R * HEADS, HD), keys_cache, value_block_cache, block_table, ctx_len, out_weight
    )


def solution(mesh):
    return jax.shard_map(
        local,
        mesh=mesh,
        in_specs=(
            P("inst", "tp", None),
            P("inst", "tp", None, None),
            P("inst", "tp", None, None),
            P("inst", None),
            P("inst"),
            P("tp", "inst"),
        ),
        out_specs=P("tp", "inst"),
        check_vma=False,
    )
```

time: 274 us -> 64.5 us (0.24)
  waiting for transfers between devices: 179 us -> 0 us
  Pallas kernels: 0 us -> 58.1 us
  starting transfers between devices: 37.8 us -> 0 us
  local copies, waits for them, and re-layouts: 24.2 us -> 6.19 us
  between operations: 13.4 us -> 0.01 us
  matrix products: 13.2 us -> 0 us
  other arithmetic: 4.21 us -> 0 us
    all_gather x2 -> x0, waiting for transfers between devices: 114 us -> none  [the longest x1 74.8 us: local(): lax.all_gather(attention, 'inst', axis=0, tiled=True)]
    pallas_call x0 -> x1, Pallas kernels: none -> 58.1 us  [local(): pl.pallas_call(kernel, out_shape=jax.ShapeDtypeStruct((N_INST * R // TP,...]
    all_to_all x5 -> x0, waiting for transfers between devices: 46.3 us -> none  [the longest x1 26.9 us: local(): lax.all_to_all(lent_rows(block_out), 'inst', split_axis=0, concat_axis=0,...]
    all_to_all x5 -> x0, starting transfers between devices: 37.7 us -> none  [the longest x1 13 us: local(): lax.all_to_all(slot_valid.reshape(inst_count, reserved), 'inst', split_ax...]
    reduce_scatter x1 -> x0, waiting for transfers between devices: 18.4 us -> none  [local(): mixed = lax.psum_scatter(terms, 'tp', scatter_dimension=0, tiled=True)]
    dot_general x4 -> x0, matrix products: 13.2 us -> none  [the longest x1 4.82 us: local(): jnp.einsum('pkgd,pktd->pkgt', query_groups, keys_cache, preferred_element...]
    scatter x4 -> x0, local copies, waits for them, and re-layouts: 11.6 us -> none  [the longest x2 5.83 us: local(): jnp.zeros((home_pages,), jnp.int32).at[home_slot]]
    gather x7 -> x0, local copies, waits for them, and re-layouts: 8.98 us -> none  [the longest x3 4.15 us: lent_rows(): return padded[page_home]]
  transfers between devices with their start and end apart: 8 -> 0, of which waited for: 8 -> 0; matrix products, arithmetic and copies ran while one was open for 9% -> 0% of each run, Pallas kernels for 0% -> 0%
where the time goes in v1:
time: 64.5 us; the launch traced here: 64.3 us
  Pallas kernels  58.1 us (90%)
  local copies, waits for them, and re-layouts  6.19 us (10%)
    pallas_call x1, Pallas kernels, local(): pl.pallas_call(kernel, out_shape=jax.ShapeDtypeStruct((N_INST * R // TP,...  58.1 us
    unnamed x11, local copies, waits for them, and re-layouts  6.19 us

profile of v1, /device:TPU:1, one launch (start us, length us, event | category | flops | bytes accessed | tf_op | source)
XLA Modules:
  0.0 64.3 jit_solution(17226076410623455195)
XLA Ops:
  0.0 0.0 copy-start
  0.0 2.4 %copy-done = bf16[154,2,64,128]{3,2,1,0:T(8,128)(2,1)S(1)} copy-done((bf16[154,2,64,128]{3,2,1,0:T(8,128)(2,1)S(1)}, bf16[154,2,64,128]{3,2,1,0:T(8,128)(2,1)}, u32[]{:S(2)}) %copy-start) | copy-done | bytes 5046296
  2.4 0.0 copy-start.1
  2.4 1.0 %copy-done.1 = bf16[2048,128]{1,0:T(8,128)(2,1)S(1)} copy-done((bf16[2048,128]{1,0:T(8,128)(2,1)S(1)}, bf16[2048,128]{1,0:T(8,128)(2,1)}, u32[]{:S(2)}) %copy-start.1) | copy-done | bytes 524312
  3.5 0.0 copy-start.2
  3.5 0.8 %copy-done.2 = bf16[8,16,128]{2,1,0:T(8,128)(2,1)S(1)} copy-done((bf16[8,16,128]{2,1,0:T(8,128)(2,1)S(1)}, bf16[8,16,128]{2,1,0:T(8,128)(2,1)}, u32[]{:S(2)}) %copy-start.2) | copy-done | bytes 32792
  4.2 0.0 copy-start.3
  4.2 0.7 %copy-done.3 = s32[8,48]{1,0:T(8,128)S(1)} copy-done((s32[8,48]{1,0:T(8,128)S(1)}, s32[8,48]{1,0:T(8,128)}, u32[]{:S(2)}) %copy-start.3) | copy-done | bytes 1560
  4.9 0.0 copy-start.4
  4.9 0.7 %copy-done.4 = s32[8]{0:T(128)S(1)} copy-done((s32[8]{0:T(128)S(1)}, s32[8]{0:T(128)}, u32[]{:S(2)}) %copy-start.4) | copy-done | bytes 56
  5.6 58.1 %paged_decode.1 = bf16[128,128]{1,0:T(8,128)(2,1)S(1)} custom-call(bf16[128,128]{1,0:T(8,128)(2,1)S(1)} %bitcast.1, bf16[154,2,64,128]{3,2,1,0:T(8,128)(2,1)S(1)} %copy-done, bf16[154,2,64,128]{3,2,1,0:T(8,128)(2,1)} %v_hbm.1, s32[8,48]{1,0:T(8,128)S(1)} %copy-done.3, s32[8]{0:T(128)S(1)} %copy-done.4, bf16[2048,128]{1,0:T(8,128)(2,1)S(1)} %copy-done.1), custom_call_target="tpu_custom_call" | custom-call | tf_op jit(solution)/shard_map/paged_decode/pallas_call | solution.py:321
  63.6 0.6 copy.8
Async XLA Ops:
  0.0 2.4 %copy-start = (bf16[154,2,64,128]{3,2,1,0:T(8,128)(2,1)S(1)}, bf16[154,2,64,128]{3,2,1,0:T(8,128)(2,1)}, u32[]{:S(2)}) copy-start(bf16[154,2,64,128]{3,2,1,0:T(8,128)(2,1)} %k_hbm.1) | copy-start | bytes 15138820
  2.4 1.0 %copy-start.1 = (bf16[2048,128]{1,0:T(8,128)(2,1)S(1)}, bf16[2048,128]{1,0:T(8,128)(2,1)}, u32[]{:S(2)}) copy-start(bf16[2048,128]{1,0:T(8,128)(2,1)} %w_hbm.1) | copy-start | bytes 1572868
  3.5 0.8 %copy-start.2 = (bf16[8,16,128]{2,1,0:T(8,128)(2,1)S(1)}, bf16[8,16,128]{2,1,0:T(8,128)(2,1)}, u32[]{:S(2)}) copy-start(bf16[8,16,128]{2,1,0:T(8,128)(2,1)} %param.6) | copy-start | bytes 98308
  4.2 0.7 %copy-start.3 = (s32[8,48]{1,0:T(8,128)S(1)}, s32[8,48]{1,0:T(8,128)}, u32[]{:S(2)}) copy-start(s32[8,48]{1,0:T(8,128)} %tab_ref.1) | copy-start | bytes 4612
  4.9 0.7 %copy-start.4 = (s32[8]{0:T(128)S(1)}, s32[8]{0:T(128)}, u32[]{:S(2)}) copy-start(s32[8]{0:T(128)} %ctx_ref.1) | copy-start | bytes 100

commit v2 on v1

v2 whole, which is shorter than its diff:
```python
import math

import jax
import jax.numpy as jnp
from jax import lax
from jax.experimental import pallas as pl
from jax.experimental.pallas import tpu as pltpu
from jax.sharding import PartitionSpec as P

MESH = pl.DeviceIdType.MESH
F32 = jnp.float32
BF16 = jnp.bfloat16

N_INST = 64
TP = 4
ZN, XN = 8, 4
R = 8
HEADS = 16
KV = 2
GROUP = HEADS // KV
HD = 128
BT = 64
CAP = 2
PAGES = 154
HOME = PAGES - CAP * (N_INST - 1)
OTHERB = 4
MAXB = 48
LOW = -1e30
SCALE = math.log2(math.e) / math.sqrt(HD)
ORDER = (0, 1, 7, 2, 6, 3, 5, 4)
NEAR = ORDER[1:]
BATCHES = ((1, 2), (3, 2), (5, 3))


def iota(shape, dim):
    return lax.broadcasted_iota(jnp.int32, shape, dim)


def dot(a, b):
    return jnp.dot(a, b, preferred_element_type=F32)


def dot_t(a, b):
    return lax.dot_general(a, b, (((1,), (1,)), ((), ())), preferred_element_type=F32)


def remote(src, dst, send, recv, where):
    return pltpu.make_async_remote_copy(
        src_ref=src, dst_ref=dst, send_sem=send, recv_sem=recv, device_id=where, device_id_type=MESH
    )


def drain(ref, sem):
    pltpu.make_async_copy(ref, ref, sem).wait()


def kernel(
    q_hbm, k_hbm, v_hbm, tab_hbm, ctx_hbm, w_hbm, out_ref,
    q_buf, tab_buf, ctx_buf, kbuf, vbuf, wbuf, qall, meta, abuf,
    rsend, rrecv, ssend, srecv, r2send, r2recv, s2send, s2recv,
    a2, a2f, own, ysend, yrecv, y2send, y2recv,
    ld, qs, ms, qr, mr, zqr, zmr, zs, zr, xs, xr, cs, cr, rs, rr, ss, sr, r2s, r2r, s2s, s2r,
    gs, gr, zgr, ys, yr, y2s, y2r,
):
    me = lax.axis_index("inst")
    tp = lax.axis_index("tp")
    z, xc = me // 8, me % 8
    x, c = xc // 2, xc % 2

    barrier = pltpu.get_barrier_semaphore()

    others = [{"inst": ((z + d) & 7) * 8 + xc} for d in NEAR]
    others += [{"inst": z * 8 + ((xc + e) & 7)} for e in range(1, 8)]
    others += [{"tp": (tp + d) % TP} for d in range(1, TP)]
    for where in others:
        pl.semaphore_signal(barrier, inc=1, device_id=where, device_id_type=MESH)

    half = HEADS * HD // 2
    small = [
        pltpu.make_async_copy(ctx_hbm, ctx_buf, ld.at[6]),
        pltpu.make_async_copy(tab_hbm, tab_buf, ld.at[7]),
        pltpu.make_async_copy(q_hbm, q_buf, ld.at[8]),
    ]
    loads = [
        pltpu.make_async_copy(k_hbm.at[pl.ds(0, HOME)], kbuf.at[pl.ds(0, HOME)], ld.at[0]),
        pltpu.make_async_copy(v_hbm.at[pl.ds(0, HOME)], vbuf.at[pl.ds(0, HOME)], ld.at[1]),
        pltpu.make_async_copy(k_hbm.at[pl.ds(HOME, PAGES - HOME)], kbuf.at[pl.ds(HOME, PAGES - HOME)], ld.at[2]),
        pltpu.make_async_copy(v_hbm.at[pl.ds(HOME, PAGES - HOME)], vbuf.at[pl.ds(HOME, PAGES - HOME)], ld.at[3]),
        pltpu.make_async_copy(w_hbm.at[pl.ds(0, half)], wbuf.at[0], ld.at[4]),
        pltpu.make_async_copy(w_hbm.at[pl.ds(half, half)], wbuf.at[1], ld.at[5]),
    ]
    for copy in small + loads:
        copy.start()
    for copy in small:
        copy.wait()

    tab = tab_buf[...]
    row8, lane8 = iota((R, 128), 0), iota((R, 128), 1)
    ctx = jnp.zeros((R, 1), jnp.int32)
    for n in range(R):
        ctx = jnp.where(iota((R, 1), 0) == n, ctx_buf[n], ctx)
    lender, slot = lane8 >> 1, lane8 & 1
    target = lender * PAGES + HOME + (((lender - me) & (N_INST - 1)) - 1) * CAP + slot
    target = jnp.where(lender == me, -5, target)
    slots = jnp.zeros((R, 128), jnp.int32)
    home = jnp.zeros((R, 128), jnp.int32)
    for b in range(MAXB):
        valid = jnp.clip(ctx - b * BT, 0, BT)
        page = tab[:, b : b + 1]
        slots = slots + jnp.where(page == target, valid, 0)
        if b < OTHERB:
            home = home + jnp.where(page == me * PAGES + lane8, valid, 0)
    longest = jnp.sum(jnp.where(ctx > OTHERB * BT, iota((R, 1), 0), 0).astype(F32), axis=0, keepdims=True)
    slots = jnp.sum(slots.astype(F32), axis=0, keepdims=True)
    slots = jnp.where(lane8[0:1] == 2 * me, longest, slots)
    meta[0, xc] = slots.astype(jnp.int32)
    q = q_buf[...]
    pick = iota((HEADS, 128), 1).astype(F32) == longest * HEADS + iota((HEADS, 128), 0).astype(F32)
    qall[0, xc] = dot(pick.astype(F32).astype(BF16), q).astype(BF16)

    prow, plane = iota((128, 128), 0), iota((128, 128), 1)
    perm = plane == (prow & 7) * HEADS + (prow >> 6) * GROUP + ((prow >> 3) & 7)
    qp = dot(perm.astype(F32).astype(BF16), q).astype(BF16)
    tokens = HOME * BT
    spread = (iota((128, tokens), 1) >> 6) == iota((128, tokens), 0)
    vtok = dot(home.astype(F32).astype(BF16), spread.astype(F32).astype(BF16))
    bias = jnp.where((iota((R, tokens), 1) & (BT - 1)).astype(F32) < vtok, 0.0, LOW)
    loads[0].wait()
    loads[1].wait()
    short = iota((R, 1), 0).astype(F32) != longest
    outs = []
    for k in range(KV):
        keys = kbuf[pl.ds(0, HOME), k].reshape(tokens, HD)
        values = vbuf[pl.ds(0, HOME), k].reshape(tokens, HD)
        s = dot_t(qp[k * 64 : (k + 1) * 64], keys).reshape(GROUP, R, tokens) * SCALE + bias[None]
        top = jnp.max(s, axis=-1, keepdims=True)
        p = jnp.exp2(s - top)
        total = jnp.sum(p, axis=-1, keepdims=True)
        o = dot(p.reshape(64, tokens).astype(BF16), values).reshape(GROUP, R, HD)
        outs.append(jnp.where(short[None], o / total, 0.0))
    for g in range(GROUP):
        abuf[me, :, g * HD : (g + 1) * HD] = jnp.concatenate([outs[0][g], outs[1][g]], axis=0).astype(BF16)

    pl.semaphore_wait(barrier, len(others))

    def along_z(ref, send, recv):
        for i in (7, 5, 6, 3, 4, 1, 2):
            remote(ref.at[0, xc], ref.at[i, xc], send, recv.at[i], {"inst": ((z + ORDER[i]) & 7) * 8 + xc}).start()

    def around(ref, first, count, send, recv):
        block = ref.at[pl.ds(first, count), xc]
        for e in range(1, 8):
            remote(block, block, send, recv, {"inst": z * 8 + ((xc + e) & 7)}).start()

    def relay_q(batch):
        first, count = BATCHES[batch]
        for i in range(first, first + count):
            drain(qall.at[0, 0], zqr.at[i])
            drain(meta.at[0, 0], zmr.at[i])
        around(qall, first, count, qs, qr.at[batch])
        around(meta, first, count, ms, mr.at[batch])

    along_z(qall, qs, zqr)
    along_z(meta, ms, zmr)
    around(qall, 0, 1, qs, qr.at[3])
    around(meta, 0, 1, ms, mr.at[3])

    sib = {"inst": me + 1 - 2 * c}
    copies = {}

    def pass_z(dz, step):
        block = abuf.at[((z - dz) & 7) * 8 + xc]
        slot = (dz + step) & 7
        copies["z", slot] = remote(block, block, zs.at[slot], zr.at[slot], {"inst": ((z + step) & 7) * 8 + xc})
        copies["z", slot].start()

    def take(kind, *key):
        copies[(kind,) + key].wait_recv()

    def pass_x(dz, dx, step):
        block = abuf.at[((z - dz) & 7) * 8 + ((x - dx) & 3) * 2 + c]
        to = (dx + step) & 3
        slot = 4 * dz + to
        copies["x", dz, to] = remote(
            block, block, xs.at[slot], xr.at[slot], {"inst": z * 8 + ((x + step) & 3) * 2 + c}
        )
        copies["x", dz, to].start()

    def across(dz, dx):
        block = abuf.at[((z - dz) & 7) * 8 + ((x - dx) & 3) * 2 + c]
        slot = 4 * dz + dx
        copies["c", dz, dx] = remote(block, block, cs.at[slot], cr.at[slot], sib)
        copies["c", dz, dx].start()

    def start_x(*dzs):
        for dz in dzs:
            pass_x(dz, 0, 1)
            pass_x(dz, 0, -1)
            across(dz, 0)

    def relay_x(*dzs):
        for dz in dzs:
            take("x", dz, 1)
            take("x", dz, 3)
            if dz % 2 == 0:
                pass_x(dz, 1, 1)
            else:
                pass_x(dz, 3, -1)
            across(dz, 1)
            across(dz, 3)

    pass_z(0, 1)
    pass_z(0, -1)

    kv_of = (iota((HEADS, 256), 1) >> 6) & 1
    kv_bias = jnp.where(kv_of == iota((HEADS, 256), 0) // GROUP, 0.0, LOW)
    lane256 = iota((8, 256), 1)
    diag = iota((HEADS, 128), 1) == iota((HEADS, 128), 0)
    diag16 = iota((HEADS, 128), 1) == iota((HEADS, 128), 0) + HEADS
    loads[2].wait()
    loads[3].wait()

    def lend(i, zh, out, stats_out):
        rows = meta[i].reshape(8, 128)
        v = [jnp.sum(jnp.where(lane8 == 2 * me + s, rows, 0).astype(F32), axis=-1, keepdims=True) for s in range(CAP)]
        limit = jnp.where(lane256 < 128, v[0], v[1])
        limit = jnp.where(iota((8, 256), 0) == me - zh * 8, 0.0, limit)
        bias8 = jnp.where((lane256 & (BT - 1)).astype(F32) < limit, 0.0, LOW)
        pages = [HOME - CAP + CAP * ((me - (zh * 8 + e)) & (N_INST - 1)) for e in range(8)]
        scores = [
            dot_t(qall[i, e], kbuf[pl.ds(pages[e], CAP)].reshape(256, HD)) * SCALE
            + (bias8[e : e + 1] + kv_bias)
            for e in range(8)
        ]
        for e in range(8):
            top = jnp.maximum(jnp.max(scores[e], axis=-1, keepdims=True), -1e20)
            p = jnp.exp2(scores[e] - top)
            total = jnp.sum(p, axis=-1, keepdims=True)
            o = dot(p.astype(BF16), vbuf[pl.ds(pages[e], CAP)].reshape(256, HD))
            stats = jnp.where(diag, top, jnp.where(diag16, total, 0.0))
            stats_out[i, e] = jnp.sum(stats, axis=0, keepdims=True)
            out[i, e] = o.astype(BF16)

    def near(i):
        step = (i + 1) // 2
        return (step * (1 - 2 * ((i + 1) % 2))) & (ZN - 1)

    def lend_z(i, carry):
        zh = (z - near(i)) & 7
        lend(i, zh, rsend, ssend)
        remote(rsend.at[i], rrecv.at[i], rs, rr, {"inst": zh * 8 + xc}).start()
        remote(ssend.at[i], srecv.at[i], ss, sr, {"inst": zh * 8 + xc}).start()
        return carry

    def wait_q(batch):
        first, count = BATCHES[batch]
        drain(qall.at[pl.ds(0, count), pl.ds(0, 7)], qr.at[batch])
        drain(meta.at[pl.ds(0, count), pl.ds(0, 7)], mr.at[batch])

    relay_q(0)
    relay_q(1)
    take("z", 1)
    pass_z(1, 1)
    take("z", 7)
    pass_z(7, -1)
    drain(qall.at[0, pl.ds(0, 7)], qr.at[3])
    drain(meta.at[0, pl.ds(0, 7)], mr.at[3])
    lend(0, z, rrecv, srecv)
    relay_q(2)
    start_x(0, 1, 7)
    take("z", 2)
    pass_z(2, 1)
    take("z", 6)
    pass_z(6, -1)
    for batch, (first, count) in enumerate(BATCHES):
        wait_q(batch)
        lax.fori_loop(first, first + count, lend_z, 0)
        if batch == 0:
            take("z", 3)
            pass_z(3, 1)
            start_x(2, 6)
    take("z", 5)
    start_x(3, 5)
    take("z", 4)
    start_x(4)
    relay_x(0, 1, 7, 2, 6)

    lanes = iota((1, 128), 1)
    drain(srecv.at[pl.ds(0, 7)], sr)
    stats = srecv[...].reshape(8, 8, 128)
    best = jnp.max(stats, axis=0)
    share = jnp.exp2(stats - best[None])
    den = jnp.sum(share * pltpu.roll(stats.reshape(64, 128), 128 - HEADS, 1).reshape(8, 8, 128), axis=0)
    totals = pltpu.roll(den, HEADS, 1)
    share = jnp.concatenate([share.reshape(64, 128), jnp.zeros((64, 128), F32)], axis=0).T[:HEADS]
    merged = jnp.where(lanes < HEADS, best, jnp.where(lanes < 2 * HEADS, totals, 0.0))
    for e in range(8):
        s2send[e] = merged[e : e + 1]
    drain(rrecv.at[pl.ds(0, 7)], rr)
    for e in range(8):
        terms = [share[:, i * 8 + e : i * 8 + e + 1] * rrecv[i, e].astype(F32) for i in range(8)]
        r2send[e] = (((terms[0] + terms[1]) + (terms[2] + terms[3])) + ((terms[4] + terms[5]) + (terms[6] + terms[7]))).astype(BF16)
    for e in range(1, 8):
        to = (xc + e) & 7
        remote(s2send.at[to], s2recv.at[e], s2s, s2r, {"inst": z * 8 + to}).start()
        remote(r2send.at[to], r2recv.at[e], r2s, r2r, {"inst": z * 8 + to}).start()
    relay_x(3, 5, 4)
    s2recv[0] = s2send[xc]
    r2recv[0] = r2send[xc]
    drain(s2recv.at[pl.ds(0, 7)], s2r)
    stats = s2recv[...].reshape(8, 128)
    share = jnp.exp2(stats - jnp.max(stats, axis=0, keepdims=True))
    den = jnp.sum(share * pltpu.roll(stats, 128 - HEADS, 1), axis=0, keepdims=True)
    share = share / jnp.where(lanes < HEADS, den, 1.0)
    share = jnp.concatenate([share, jnp.zeros((120, 128), F32)], axis=0).T[:HEADS]
    drain(r2recv.at[pl.ds(0, 7)], r2r)
    terms = [share[:, i : i + 1] * r2recv[i].astype(F32) for i in range(8)]
    a2[0, xc] = (((terms[0] + terms[1]) + (terms[2] + terms[3])) + ((terms[4] + terms[5]) + (terms[6] + terms[7]))).astype(BF16)

    along_z(a2, gs, zgr)
    around(a2, 0, 1, gs, gr.at[3])

    def relay_a2(batch):
        first, count = BATCHES[batch]
        for i in range(first, first + count):
            drain(a2.at[0, 0], zgr.at[i])
        around(a2, first, count, gs, gr.at[batch])

    for dz in ORDER:
        take("x", dz, 2)
        across(dz, 2)
    loads[4].wait()
    loads[5].wait()
    for dz in ORDER:
        for dx in range(XN):
            take("c", dz, dx)

    def project(i, carry):
        a = abuf[pl.ds(i * 16, 16)].reshape(256, half)
        t0 = dot(a, wbuf[0]).reshape(16, 16, HD)
        t1 = dot(a, wbuf[1]).reshape(16, 16, HD)
        ysend[i] = (t0[:, 0:8] + t1[:, 8:16]).reshape(128, HD)
        return carry

    lax.fori_loop(0, TP, project, 0)
    ycopies = []
    for d in range(1, TP):
        to = (tp + d) % TP
        ycopies.append(remote(ysend.at[to], yrecv.at[d], ys.at[d], yr.at[d], {"tp": to}))
        ycopies[-1].start()

    relay_a2(0)
    relay_a2(1)
    relay_a2(2)

    for i in range(8):
        zh = (z - ORDER[i]) & 7
        mine = lane8 == 2 * (zh * 8 + row8)
        owner = jnp.sum(jnp.where(mine, meta[i].reshape(8, 128), 0).astype(F32), axis=-1, keepdims=True)
        own[zh] = jnp.broadcast_to(owner, (8, 128))
    drain(a2.at[0, pl.ds(0, 7)], gr.at[3])
    for batch, (first, count) in enumerate(BATCHES):
        drain(a2.at[pl.ds(0, count), pl.ds(0, 7)], gr.at[batch])
    a2f[...] = a2[...].astype(F32).reshape(N_INST * HEADS, HD)
    left = [a2f[pl.ds(h, N_INST, stride=HEADS), :].astype(BF16) for h in range(HEADS)]
    t2 = dot(jnp.concatenate(left[:8], axis=1), wbuf[0]) + dot(jnp.concatenate(left[8:], axis=1), wbuf[1])
    for i in range(8):
        y2send[(z - ORDER[i]) & 7] = t2[i * 8 : i * 8 + 8]
    for d in range(1, TP):
        to = (tp + d) % TP
        ycopies.append(remote(y2send.at[pl.ds(2 * to, 2)], y2recv.at[d], y2s.at[d], y2r.at[d], {"tp": to}))
        ycopies[-1].start()
    for copy in ycopies:
        copy.wait_recv()
    long = (y2send[pl.ds(2 * tp, 2)] + y2recv[1] + y2recv[2] + y2recv[3]).reshape(16, 128)
    frow = row8.astype(F32)
    owner = own[pl.ds(2 * tp, 2)].reshape(16, 128)
    added = [jnp.where(frow == owner[i : i + 1], long[i : i + 1], 0.0) for i in range(N_INST // TP)]
    out_ref[...] = (ysend[tp] + yrecv[1] + yrecv[2] + yrecv[3] + jnp.concatenate(added, axis=0)).astype(BF16)

    for copy in ycopies + list(copies.values()):
        copy.wait_send()
    for ref, sem in ((qall, qs), (meta, ms), (a2, gs)):
        drain(ref.at[pl.ds(0, 7)], sem)
        drain(ref.at[0, pl.ds(0, 7)], sem)
    for ref, sem in ((rsend, rs), (ssend, ss), (r2send, r2s), (s2send, s2s)):
        drain(ref.at[pl.ds(0, 7)], sem)


def local(queries, keys_cache, value_block_cache, block_table, ctx_len, out_weight):
    dma = pltpu.SemaphoreType.DMA
    vmem = pl.BlockSpec(memory_space=pltpu.VMEM)
    hbm = pl.BlockSpec(memory_space=pltpu.HBM)
    return pl.pallas_call(
        kernel,
        out_shape=jax.ShapeDtypeStruct((N_INST * R // TP, HD), BF16),
        in_specs=[hbm] * 6,
        out_specs=vmem,
        scratch_shapes=[
            pltpu.VMEM((R * HEADS, HD), BF16),
            pltpu.VMEM((R, MAXB), jnp.int32),
            pltpu.SMEM((R,), jnp.int32),
            pltpu.VMEM((PAGES, KV, BT, HD), BF16),
            pltpu.VMEM((PAGES, KV, BT, HD), BF16),
            pltpu.VMEM((2, HEADS * HD // 2, HD), BF16),
            pltpu.VMEM((8, 8, HEADS, HD), BF16),
            pltpu.VMEM((8, 8, 1, 128), jnp.int32),
            pltpu.VMEM((N_INST, HEADS, GROUP * HD), BF16),
            pltpu.VMEM((8, 8, HEADS, HD), BF16),
            pltpu.VMEM((8, 8, HEADS, HD), BF16),
            pltpu.VMEM((8, 8, 1, 128), F32),
            pltpu.VMEM((8, 8, 1, 128), F32),
            pltpu.VMEM((8, HEADS, HD), BF16),
            pltpu.VMEM((8, HEADS, HD), BF16),
            pltpu.VMEM((8, 1, 128), F32),
            pltpu.VMEM((8, 1, 128), F32),
            pltpu.VMEM((8, 8, HEADS, HD), BF16),
            pltpu.VMEM((N_INST * HEADS, HD), F32),
            pltpu.VMEM((8, 8, 128), F32),
            pltpu.VMEM((TP, N_INST * R // TP, HD), F32),
            pltpu.VMEM((TP, N_INST * R // TP, HD), F32),
            pltpu.VMEM((8, 8, HD), F32),
            pltpu.VMEM((TP, 2, 8, HD), F32),
            dma((9,)),
            dma, dma, dma((4,)), dma((4,)), dma((ZN,)), dma((ZN,)),
            dma((ZN,)), dma((ZN,)),
            dma((4 * ZN,)), dma((4 * ZN,)),
            dma((4 * ZN,)), dma((4 * ZN,)),
            dma, dma, dma, dma,
            dma, dma, dma, dma,
            dma, dma((4,)), dma((ZN,)),
            dma((TP,)), dma((TP,)),
            dma((TP,)), dma((TP,)),
        ],
        name="paged_decode",
        compiler_params=pltpu.CompilerParams(
            collective_id=0, has_side_effects=True, vmem_limit_bytes=60 * 2**20
        ),
    )(
        queries.reshape(R * HEADS, HD), keys_cache, value_block_cache, block_table, ctx_len, out_weight
    )


def solution(mesh):
    return jax.shard_map(
        local,
        mesh=mesh,
        in_specs=(
            P("inst", "tp", None),
            P("inst", "tp", None, None),
            P("inst", "tp", None, None),
            P("inst", None),
            P("inst"),
            P("tp", "inst"),
        ),
        out_specs=P("tp", "inst"),
        check_vma=False,
    )
```

time: 64.5 us -> 49.5 us (0.77)
  Pallas kernels: 58.1 us -> 48 us
  local copies, waits for them, and re-layouts: 6.19 us -> 1.38 us
    pallas_call x1, Pallas kernels: 58.1 us -> 48 us  [local(): pl.pallas_call(kernel, out_shape=jax.ShapeDtypeStruct((N_INST * R // TP,...]
    unnamed x11 -> x1, local copies, waits for them, and re-layouts: 6.19 us -> 1.38 us
where the time goes in v2:
time: 49.5 us; the launch traced here: 49.4 us
  Pallas kernels  48 us (97%)
  local copies, waits for them, and re-layouts  1.38 us (3%)
    pallas_call x1, Pallas kernels, local(): pl.pallas_call(kernel, out_shape=jax.ShapeDtypeStruct((N_INST * R // TP,...  48 us
    unnamed x1, local copies, waits for them, and re-layouts  1.38 us

profile of v2, /device:TPU:1, one launch (start us, length us, event | category | flops | bytes accessed | tf_op | source)
XLA Modules:
  0.0 49.4 jit_solution(14686461322290627269)
XLA Ops:
  0.0 48.0 %paged_decode.1 = bf16[128,128]{1,0:T(8,128)(2,1)} custom-call(bf16[128,128]{1,0:T(8,128)(2,1)} %bitcast.1, bf16[154,2,64,128]{3,2,1,0:T(8,128)(2,1)} %k_hbm.1, bf16[154,2,64,128]{3,2,1,0:T(8,128)(2,1)} %v_hbm.1, s32[8,48]{1,0:T(8,128)} %tab_hbm.1, s32[8]{0:T(128)} %ctx_hbm.1, bf16[2048,128]{1,0:T(8,128)(2,1)} %w_hbm.1), custom_call_target="tpu_custom_call" | custom-call | tf_op jit(solution)/shard_map/paged_decode/pallas_call | solution.py:394
  48.0 1.4 %copy.8 = bf16[128,128]{1,0:T(8,128)(2,1)} copy(bf16[128,128]{1,0:T(8,128)(2,1)} %paged_decode.1) | data formatting | bytes 65536

commit v3 on v2

--- a/solution.py
+++ b/solution.py
@@ -27,8 +27,13 @@
 MAXB = 48
 LOW = -1e30
 SCALE = math.log2(math.e) / math.sqrt(HD)
-ORDER = (0, 1, 7, 2, 6, 3, 5, 4)
+ORDER = (0, 1, 7, 2, 6, 4, 3, 5)
 NEAR = ORDER[1:]
+FAR = sorted(
+    ((i, dx, dc) for i in range(8) for dx in range(4) for dc in range(2) if (i, dx, dc) != (0, 0, 0)),
+    key=lambda t: -(min(ORDER[t[0]], 8 - ORDER[t[0]]) + min(t[1], 4 - t[1]) + t[2]),
+)
+AROUND = ((2, 1), (2, 0), (1, 1), (3, 1), (1, 0), (3, 0), (0, 1), (0, 0))
 BATCHES = ((1, 2), (3, 2), (5, 3))
 
 
@@ -57,16 +62,24 @@
 def kernel(
     q_hbm, k_hbm, v_hbm, tab_hbm, ctx_hbm, w_hbm, out_ref,
     q_buf, tab_buf, ctx_buf, kbuf, vbuf, wbuf, qall, meta, abuf,
-    rsend, rrecv, ssend, srecv, r2send, r2recv, s2send, s2recv,
+    rsend, rrecv, ssend, srecv,
     a2, a2f, own, ysend, yrecv, y2send, y2recv,
-    ld, qs, ms, qr, mr, zqr, zmr, zs, zr, xs, xr, cs, cr, rs, rr, ss, sr, r2s, r2r, s2s, s2r,
-    gs, gr, zgr, ys, yr, y2s, y2r,
+    ld, qs, ms, qr, mr, zqr, zmr, zs, zr, xs, xr, cs, cr, rs, rr, ss, sr,
+    gs, gr, ys, yr, y2s, y2r,
 ):
     me = lax.axis_index("inst")
     tp = lax.axis_index("tp")
     z, xc = me // 8, me % 8
     x, c = xc // 2, xc % 2
 
+    small = [
+        pltpu.make_async_copy(ctx_hbm, ctx_buf, ld.at[6]),
+        pltpu.make_async_copy(tab_hbm, tab_buf, ld.at[7]),
+        pltpu.make_async_copy(q_hbm, q_buf, ld.at[8]),
+    ]
+    for copy in small:
+        copy.start()
+
     barrier = pltpu.get_barrier_semaphore()
 
     others = [{"inst": ((z + d) & 7) * 8 + xc} for d in NEAR]
@@ -76,11 +89,6 @@
         pl.semaphore_signal(barrier, inc=1, device_id=where, device_id_type=MESH)
 
     half = HEADS * HD // 2
-    small = [
-        pltpu.make_async_copy(ctx_hbm, ctx_buf, ld.at[6]),
-        pltpu.make_async_copy(tab_hbm, tab_buf, ld.at[7]),
-        pltpu.make_async_copy(q_hbm, q_buf, ld.at[8]),
-    ]
     loads = [
         pltpu.make_async_copy(k_hbm.at[pl.ds(0, HOME)], kbuf.at[pl.ds(0, HOME)], ld.at[0]),
         pltpu.make_async_copy(v_hbm.at[pl.ds(0, HOME)], vbuf.at[pl.ds(0, HOME)], ld.at[1]),
@@ -89,7 +97,7 @@
         pltpu.make_async_copy(w_hbm.at[pl.ds(0, half)], wbuf.at[0], ld.at[4]),
         pltpu.make_async_copy(w_hbm.at[pl.ds(half, half)], wbuf.at[1], ld.at[5]),
     ]
-    for copy in small + loads:
+    for copy in loads:
         copy.start()
     for copy in small:
         copy.wait()
@@ -118,6 +126,74 @@
     pick = iota((HEADS, 128), 1).astype(F32) == longest * HEADS + iota((HEADS, 128), 0).astype(F32)
     qall[0, xc] = dot(pick.astype(F32).astype(BF16), q).astype(BF16)
 
+    pl.semaphore_wait(barrier, len(others))
+
+    def along_z(ref, send, recv):
+        for i in (5, 6, 7, 3, 4, 1, 2):
+            remote(ref.at[0, xc], ref.at[i, xc], send, recv.at[i], {"inst": ((z + ORDER[i]) & 7) * 8 + xc}).start()
+
+    def around(ref, first, count, send, recv):
+        block = ref.at[pl.ds(first, count), xc]
+        for e in range(1, 8):
+            remote(block, block, send, recv, {"inst": z * 8 + ((xc + e) & 7)}).start()
+
+    def relay_q(batch):
+        first, count = BATCHES[batch]
+        for i in range(first, first + count):
+            drain(qall.at[0, 0], zqr.at[i])
+            drain(meta.at[0, 0], zmr.at[i])
+        around(qall, first, count, qs, qr.at[batch])
+        around(meta, first, count, ms, mr.at[batch])
+
+    along_z(qall, qs, zqr)
+    along_z(meta, ms, zmr)
+    around(qall, 0, 1, qs, qr.at[3])
+    around(meta, 0, 1, ms, mr.at[3])
+
+    sib = {"inst": me + 1 - 2 * c}
+    copies = {}
+
+    def pass_z(dz, step):
+        block = abuf.at[((z - dz) & 7) * 8 + xc]
+        slot = (dz + step) & 7
+        copies["z", slot] = remote(block, block, zs.at[slot], zr.at[slot], {"inst": ((z + step) & 7) * 8 + xc})
+        copies["z", slot].start()
+
+    def take(kind, *key):
+        copies[(kind,) + key].wait_recv()
+
+    def pass_x(dz, dx, step):
+        block = abuf.at[((z - dz) & 7) * 8 + ((x - dx) & 3) * 2 + c]
+        to = (dx + step) & 3
+        slot = 4 * dz + to
+        copies["x", dz, to] = remote(
+            block, block, xs.at[slot], xr.at[slot], {"inst": z * 8 + ((x + step) & 3) * 2 + c}
+        )
+        copies["x", dz, to].start()
+
+    def across(dz, dx):
+        block = abuf.at[((z - dz) & 7) * 8 + ((x - dx) & 3) * 2 + c]
+        slot = 4 * dz + dx
+        copies["c", dz, dx] = remote(block, block, cs.at[slot], cr.at[slot], sib)
+        copies["c", dz, dx].start()
+
+    def start_x(*dzs):
+        for dz in dzs:
+            pass_x(dz, 0, 1)
+            pass_x(dz, 0, -1)
+            across(dz, 0)
+
+    def relay_x(*dzs):
+        for dz in dzs:
+            take("x", dz, 1)
+            take("x", dz, 3)
+            if dz % 2 == 0:
+                pass_x(dz, 1, 1)
+            else:
+                pass_x(dz, 3, -1)
+            across(dz, 1)
+            across(dz, 3)
+
     prow, plane = iota((128, 128), 0), iota((128, 128), 1)
     perm = plane == (prow & 7) * HEADS + (prow >> 6) * GROUP + ((prow >> 3) & 7)
     qp = dot(perm.astype(F32).astype(BF16), q).astype(BF16)
@@ -141,74 +217,6 @@
     for g in range(GROUP):
         abuf[me, :, g * HD : (g + 1) * HD] = jnp.concatenate([outs[0][g], outs[1][g]], axis=0).astype(BF16)
 
-    pl.semaphore_wait(barrier, len(others))
-
-    def along_z(ref, send, recv):
-        for i in (7, 5, 6, 3, 4, 1, 2):
-            remote(ref.at[0, xc], ref.at[i, xc], send, recv.at[i], {"inst": ((z + ORDER[i]) & 7) * 8 + xc}).start()
-
-    def around(ref, first, count, send, recv):
-        block = ref.at[pl.ds(first, count), xc]
-        for e in range(1, 8):
-            remote(block, block, send, recv, {"inst": z * 8 + ((xc + e) & 7)}).start()
-
-    def relay_q(batch):
-        first, count = BATCHES[batch]
-        for i in range(first, first + count):
-            drain(qall.at[0, 0], zqr.at[i])
-            drain(meta.at[0, 0], zmr.at[i])
-        around(qall, first, count, qs, qr.at[batch])
-        around(meta, first, count, ms, mr.at[batch])
-
-    along_z(qall, qs, zqr)
-    along_z(meta, ms, zmr)
-    around(qall, 0, 1, qs, qr.at[3])
-    around(meta, 0, 1, ms, mr.at[3])
-
-    sib = {"inst": me + 1 - 2 * c}
-    copies = {}
-
-    def pass_z(dz, step):
-        block = abuf.at[((z - dz) & 7) * 8 + xc]
-        slot = (dz + step) & 7
-        copies["z", slot] = remote(block, block, zs.at[slot], zr.at[slot], {"inst": ((z + step) & 7) * 8 + xc})
-        copies["z", slot].start()
-
-    def take(kind, *key):
-        copies[(kind,) + key].wait_recv()
-
-    def pass_x(dz, dx, step):
-        block = abuf.at[((z - dz) & 7) * 8 + ((x - dx) & 3) * 2 + c]
-        to = (dx + step) & 3
-        slot = 4 * dz + to
-        copies["x", dz, to] = remote(
-            block, block, xs.at[slot], xr.at[slot], {"inst": z * 8 + ((x + step) & 3) * 2 + c}
-        )
-        copies["x", dz, to].start()
-
-    def across(dz, dx):
-        block = abuf.at[((z - dz) & 7) * 8 + ((x - dx) & 3) * 2 + c]
-        slot = 4 * dz + dx
-        copies["c", dz, dx] = remote(block, block, cs.at[slot], cr.at[slot], sib)
-        copies["c", dz, dx].start()
-
-    def start_x(*dzs):
-        for dz in dzs:
-            pass_x(dz, 0, 1)
-            pass_x(dz, 0, -1)
-            across(dz, 0)
-
-    def relay_x(*dzs):
-        for dz in dzs:
-            take("x", dz, 1)
-            take("x", dz, 3)
-            if dz % 2 == 0:
-                pass_x(dz, 1, 1)
-            else:
-                pass_x(dz, 3, -1)
-            across(dz, 1)
-            across(dz, 3)
-
     pass_z(0, 1)
     pass_z(0, -1)
 
@@ -220,7 +228,7 @@
     loads[2].wait()
     loads[3].wait()
 
-    def lend(i, zh, out, stats_out):
+    def lend(i, zh):
         rows = meta[i].reshape(8, 128)
         v = [jnp.sum(jnp.where(lane8 == 2 * me + s, rows, 0).astype(F32), axis=-1, keepdims=True) for s in range(CAP)]
         limit = jnp.where(lane256 < 128, v[0], v[1])
@@ -238,18 +246,24 @@
             total = jnp.sum(p, axis=-1, keepdims=True)
             o = dot(p.astype(BF16), vbuf[pl.ds(pages[e], CAP)].reshape(256, HD))
             stats = jnp.where(diag, top, jnp.where(diag16, total, 0.0))
-            stats_out[i, e] = jnp.sum(stats, axis=0, keepdims=True)
-            out[i, e] = o.astype(BF16)
+            ssend[i, e] = jnp.sum(stats, axis=0, keepdims=True)
+            rsend[i, e] = o.astype(BF16)
 
     def near(i):
         step = (i + 1) // 2
-        return (step * (1 - 2 * ((i + 1) % 2))) & (ZN - 1)
+        return jnp.where(i < 5, (step * (1 - 2 * ((i + 1) % 2))) & (ZN - 1), jnp.where(i == 5, 4, jnp.where(i == 6, 3, 5)))
+
+    def send_r(i, zh):
+        for dx, dc in AROUND:
+            e = ((x + dx) & 3) * 2 + (c ^ dc)
+            to = {"inst": zh * 8 + e}
+            remote(ssend.at[i, e], srecv.at[i, xc], ss, sr.at[i], to).start()
+            remote(rsend.at[i, e], rrecv.at[i, xc], rs, rr.at[i], to).start()
 
     def lend_z(i, carry):
         zh = (z - near(i)) & 7
-        lend(i, zh, rsend, ssend)
-        remote(rsend.at[i], rrecv.at[i], rs, rr, {"inst": zh * 8 + xc}).start()
-        remote(ssend.at[i], srecv.at[i], ss, sr, {"inst": zh * 8 + xc}).start()
+        lend(i, zh)
+        send_r(i, zh)
         return carry
 
     def wait_q(batch):
@@ -265,7 +279,13 @@
     pass_z(7, -1)
     drain(qall.at[0, pl.ds(0, 7)], qr.at[3])
     drain(meta.at[0, pl.ds(0, 7)], mr.at[3])
-    lend(0, z, rrecv, srecv)
+    lend(0, z)
+    for dx, dc in AROUND[:-1]:
+        e = ((x + dx) & 3) * 2 + (c ^ dc)
+        remote(ssend.at[0, e], srecv.at[0, xc], ss, sr.at[0], {"inst": z * 8 + e}).start()
+        remote(rsend.at[0, e], rrecv.at[0, xc], rs, rr.at[0], {"inst": z * 8 + e}).start()
+    srecv[0, xc] = ssend[0, xc]
+    rrecv[0, xc] = rsend[0, xc]
     relay_q(2)
     start_x(0, 1, 7)
     take("z", 2)
@@ -285,46 +305,27 @@
     start_x(4)
     relay_x(0, 1, 7, 2, 6)
 
+    relay_x(3, 5, 4)
+
     lanes = iota((1, 128), 1)
-    drain(srecv.at[pl.ds(0, 7)], sr)
-    stats = srecv[...].reshape(8, 8, 128)
-    best = jnp.max(stats, axis=0)
-    share = jnp.exp2(stats - best[None])
-    den = jnp.sum(share * pltpu.roll(stats.reshape(64, 128), 128 - HEADS, 1).reshape(8, 8, 128), axis=0)
-    totals = pltpu.roll(den, HEADS, 1)
-    share = jnp.concatenate([share.reshape(64, 128), jnp.zeros((64, 128), F32)], axis=0).T[:HEADS]
-    merged = jnp.where(lanes < HEADS, best, jnp.where(lanes < 2 * HEADS, totals, 0.0))
-    for e in range(8):
-        s2send[e] = merged[e : e + 1]
-    drain(rrecv.at[pl.ds(0, 7)], rr)
-    for e in range(8):
-        terms = [share[:, i * 8 + e : i * 8 + e + 1] * rrecv[i, e].astype(F32) for i in range(8)]
-        r2send[e] = (((terms[0] + terms[1]) + (terms[2] + terms[3])) + ((terms[4] + terms[5]) + (terms[6] + terms[7]))).astype(BF16)
-    for e in range(1, 8):
-        to = (xc + e) & 7
-        remote(s2send.at[to], s2recv.at[e], s2s, s2r, {"inst": z * 8 + to}).start()
-        remote(r2send.at[to], r2recv.at[e], r2s, r2r, {"inst": z * 8 + to}).start()
-    relay_x(3, 5, 4)
-    s2recv[0] = s2send[xc]
-    r2recv[0] = r2send[xc]
-    drain(s2recv.at[pl.ds(0, 7)], s2r)
-    stats = s2recv[...].reshape(8, 128)
+    for ref, sem in ((srecv, sr), (rrecv, rr)):
+        drain(ref.at[0, pl.ds(0, 7)], sem.at[0])
+        for i in range(1, 8):
+            drain(ref.at[i], sem.at[i])
+    stats = srecv[...].reshape(64, 128)
     share = jnp.exp2(stats - jnp.max(stats, axis=0, keepdims=True))
     den = jnp.sum(share * pltpu.roll(stats, 128 - HEADS, 1), axis=0, keepdims=True)
     share = share / jnp.where(lanes < HEADS, den, 1.0)
-    share = jnp.concatenate([share, jnp.zeros((120, 128), F32)], axis=0).T[:HEADS]
-    drain(r2recv.at[pl.ds(0, 7)], r2r)
-    terms = [share[:, i : i + 1] * r2recv[i].astype(F32) for i in range(8)]
-    a2[0, xc] = (((terms[0] + terms[1]) + (terms[2] + terms[3])) + ((terms[4] + terms[5]) + (terms[6] + terms[7]))).astype(BF16)
-
-    along_z(a2, gs, zgr)
-    around(a2, 0, 1, gs, gr.at[3])
-
-    def relay_a2(batch):
-        first, count = BATCHES[batch]
-        for i in range(first, first + count):
-            drain(a2.at[0, 0], zgr.at[i])
-        around(a2, first, count, gs, gr.at[batch])
+    share = jnp.concatenate([share, jnp.zeros((64, 128), F32)], axis=0).T[:HEADS]
+    parts = []
+    for i in range(8):
+        terms = [share[:, i * 8 + e : i * 8 + e + 1] * rrecv[i, e].astype(F32) for e in range(8)]
+        parts.append(sum(terms[1:], terms[0]))
+    a2[0, xc] = sum(parts[1:], parts[0]).astype(BF16)
+
+    for i, dx, dc in FAR:
+        to = ((z + ORDER[i]) & 7) * 8 + ((x + dx) & 3) * 2 + (c ^ dc)
+        remote(a2.at[0, xc], a2.at[i, xc], gs, gr.at[i], {"inst": to}).start()
 
     for dz in ORDER:
         take("x", dz, 2)
@@ -349,18 +350,15 @@
         ycopies.append(remote(ysend.at[to], yrecv.at[d], ys.at[d], yr.at[d], {"tp": to}))
         ycopies[-1].start()
 
-    relay_a2(0)
-    relay_a2(1)
-    relay_a2(2)
 
     for i in range(8):
         zh = (z - ORDER[i]) & 7
         mine = lane8 == 2 * (zh * 8 + row8)
         owner = jnp.sum(jnp.where(mine, meta[i].reshape(8, 128), 0).astype(F32), axis=-1, keepdims=True)
         own[zh] = jnp.broadcast_to(owner, (8, 128))
-    drain(a2.at[0, pl.ds(0, 7)], gr.at[3])
-    for batch, (first, count) in enumerate(BATCHES):
-        drain(a2.at[pl.ds(0, count), pl.ds(0, 7)], gr.at[batch])
+    drain(a2.at[0, pl.ds(0, 7)], gr.at[0])
+    for i in range(1, 8):
+        drain(a2.at[i], gr.at[i])
     a2f[...] = a2[...].astype(F32).reshape(N_INST * HEADS, HD)
     left = [a2f[pl.ds(h, N_INST, stride=HEADS), :].astype(BF16) for h in range(HEADS)]
     t2 = dot(jnp.concatenate(left[:8], axis=1), wbuf[0]) + dot(jnp.concatenate(left[8:], axis=1), wbuf[1])
@@ -380,11 +378,9 @@
 
     for copy in ycopies + list(copies.values()):
         copy.wait_send()
-    for ref, sem in ((qall, qs), (meta, ms), (a2, gs)):
+    for ref, sem in ((qall, qs), (meta, ms), (rsend, rs), (ssend, ss), (a2, gs)):
         drain(ref.at[pl.ds(0, 7)], sem)
         drain(ref.at[0, pl.ds(0, 7)], sem)
-    for ref, sem in ((rsend, rs), (ssend, ss), (r2send, r2s), (s2send, s2s)):
-        drain(ref.at[pl.ds(0, 7)], sem)
 
 
 def local(queries, keys_cache, value_block_cache, block_table, ctx_len, out_weight):
@@ -393,7 +389,7 @@
     hbm = pl.BlockSpec(memory_space=pltpu.HBM)
     return pl.pallas_call(
         kernel,
-        out_shape=jax.ShapeDtypeStruct((N_INST * R // TP, HD), BF16),
+        out_shape=pltpu.VMEM((N_INST * R // TP, HD), BF16),
         in_specs=[hbm] * 6,
         out_specs=vmem,
         scratch_shapes=[
@@ -410,10 +406,6 @@
             pltpu.VMEM((8, 8, HEADS, HD), BF16),
             pltpu.VMEM((8, 8, 1, 128), F32),
             pltpu.VMEM((8, 8, 1, 128), F32),
-            pltpu.VMEM((8, HEADS, HD), BF16),
-            pltpu.VMEM((8, HEADS, HD), BF16),
-            pltpu.VMEM((8, 1, 128), F32),
-            pltpu.VMEM((8, 1, 128), F32),
             pltpu.VMEM((8, 8, HEADS, HD), BF16),
             pltpu.VMEM((N_INST * HEADS, HD), F32),
             pltpu.VMEM((8, 8, 128), F32),
@@ -426,9 +418,8 @@
             dma((ZN,)), dma((ZN,)),
             dma((4 * ZN,)), dma((4 * ZN,)),
             dma((4 * ZN,)), dma((4 * ZN,)),
-            dma, dma, dma, dma,
-            dma, dma, dma, dma,
-            dma, dma((4,)), dma((ZN,)),
+            dma, dma((ZN,)), dma, dma((ZN,)),
+            dma, dma((ZN,)),
             dma((TP,)), dma((TP,)),
             dma((TP,)), dma((TP,)),
         ],

time: 49.5 us -> 44.3 us (0.89)
  Pallas kernels: 48 us -> 43.6 us
  local copies, waits for them, and re-layouts: 1.38 us -> 0.62 us
    pallas_call x1, Pallas kernels: 48 us -> 43.6 us  [local(): pl.pallas_call(kernel, out_shape=pltpu.VMEM((N_INST * R // TP, HD), BF16)...]
    unnamed x1, local copies, waits for them, and re-layouts: 1.38 us -> 0.62 us
where the time goes in v3:
time: 44.3 us; the launch traced here: 44.2 us
  Pallas kernels  43.6 us (98%)
  local copies, waits for them, and re-layouts  0.62 us (1%)
    pallas_call x1, Pallas kernels, local(): pl.pallas_call(kernel, out_shape=pltpu.VMEM((N_INST * R // TP, HD), BF16)...  43.6 us

profile of v3, /device:TPU:1, one launch (start us, length us, event | category | flops | bytes accessed | tf_op | source)
XLA Modules:
  0.0 44.2 jit_solution(3411545045895754274)
XLA Ops:
  0.0 43.6 %paged_decode.1 = bf16[128,128]{1,0:T(8,128)(2,1)S(1)} custom-call(bf16[128,128]{1,0:T(8,128)(2,1)} %bitcast.1, bf16[154,2,64,128]{3,2,1,0:T(8,128)(2,1)} %k_hbm.1, bf16[154,2,64,128]{3,2,1,0:T(8,128)(2,1)} %v_hbm.1, s32[8,48]{1,0:T(8,128)} %tab_hbm.1, s32[8]{0:T(128)} %ctx_hbm.1, bf16[2048,128]{1,0:T(8,128)(2,1)} %w_hbm.1), custom_call_target="tpu_custom_call" | custom-call | tf_op jit(solution)/shard_map/paged_decode/pallas_call | solution.py:390
  43.6 0.6 %copy.8 = bf16[128,128]{1,0:T(8,128)(2,1)} copy(bf16[128,128]{1,0:T(8,128)(2,1)S(1)} %paged_decode.1) | data formatting | bytes 65536

commit v4 on v3

--- a/solution.py
+++ b/solution.py
@@ -34,7 +34,6 @@
     key=lambda t: -(min(ORDER[t[0]], 8 - ORDER[t[0]]) + min(t[1], 4 - t[1]) + t[2]),
 )
 AROUND = ((2, 1), (2, 0), (1, 1), (3, 1), (1, 0), (3, 0), (0, 1), (0, 0))
-BATCHES = ((1, 2), (3, 2), (5, 3))
 
 
 def iota(shape, dim):
@@ -61,7 +60,7 @@
 
 def kernel(
     q_hbm, k_hbm, v_hbm, tab_hbm, ctx_hbm, w_hbm, out_ref,
-    q_buf, tab_buf, ctx_buf, kbuf, vbuf, wbuf, qall, meta, abuf,
+    q_buf, tab_buf, ctx_buf, qpb, outs, kbuf, vbuf, wbuf, qall, meta, abuf,
     rsend, rrecv, ssend, srecv,
     a2, a2f, own, ysend, yrecv, y2send, y2recv,
     ld, qs, ms, qr, mr, zqr, zmr, zs, zr, xs, xr, cs, cr, rs, rr, ss, sr,
@@ -126,29 +125,55 @@
     pick = iota((HEADS, 128), 1).astype(F32) == longest * HEADS + iota((HEADS, 128), 0).astype(F32)
     qall[0, xc] = dot(pick.astype(F32).astype(BF16), q).astype(BF16)
 
+    prow, plane = iota((128, 128), 0), iota((128, 128), 1)
+    perm = plane == (prow & 7) * HEADS + (prow >> 6) * GROUP + ((prow >> 3) & 7)
+    qp = dot(perm.astype(F32).astype(BF16), q).astype(BF16)
+    tokens = HOME * BT
+    spread = (iota((128, tokens), 1) >> 6) == iota((128, tokens), 0)
+    vtok = dot(home.astype(F32).astype(BF16), spread.astype(F32).astype(BF16))
+    bias = jnp.where((iota((R, tokens), 1) & (BT - 1)).astype(F32) < vtok, 0.0, LOW)
+    loads[0].wait()
+    loads[1].wait()
+    short = iota((R, 1), 0).astype(F32) != longest
+    qpb[...] = qp
+
+    def own_blocks(k, carry):
+        keys = kbuf[pl.ds(0, HOME), k].reshape(tokens, HD)
+        values = vbuf[pl.ds(0, HOME), k].reshape(tokens, HD)
+        s = dot_t(qpb[pl.ds(pl.multiple_of(k * 64, 64), 64)], keys).reshape(GROUP, R, tokens) * SCALE + bias[None]
+        top = jnp.max(s, axis=-1, keepdims=True)
+        p = jnp.exp2(s - top)
+        total = jnp.sum(p, axis=-1, keepdims=True)
+        o = dot(p.reshape(64, tokens).astype(BF16), values).reshape(GROUP, R, HD)
+        outs[k] = jnp.where(short[None], o / total, 0.0)
+        return carry
+
+    lax.fori_loop(0, KV, own_blocks, 0)
+    for g in range(GROUP):
+        abuf[me, :, g * HD : (g + 1) * HD] = jnp.concatenate([outs[0, g], outs[1, g]], axis=0).astype(BF16)
+
     pl.semaphore_wait(barrier, len(others))
 
     def along_z(ref, send, recv):
         for i in (5, 6, 7, 3, 4, 1, 2):
             remote(ref.at[0, xc], ref.at[i, xc], send, recv.at[i], {"inst": ((z + ORDER[i]) & 7) * 8 + xc}).start()
 
-    def around(ref, first, count, send, recv):
-        block = ref.at[pl.ds(first, count), xc]
+    def around(ref, i, send, recv):
+        block = ref.at[i, xc]
         for e in range(1, 8):
             remote(block, block, send, recv, {"inst": z * 8 + ((xc + e) & 7)}).start()
 
-    def relay_q(batch):
-        first, count = BATCHES[batch]
-        for i in range(first, first + count):
-            drain(qall.at[0, 0], zqr.at[i])
-            drain(meta.at[0, 0], zmr.at[i])
-        around(qall, first, count, qs, qr.at[batch])
-        around(meta, first, count, ms, mr.at[batch])
+    def relay_q(i, carry):
+        drain(qall.at[0, 0], zqr.at[i])
+        drain(meta.at[0, 0], zmr.at[i])
+        around(qall, i, qs, qr.at[i])
+        around(meta, i, ms, mr.at[i])
+        return carry
 
     along_z(qall, qs, zqr)
     along_z(meta, ms, zmr)
-    around(qall, 0, 1, qs, qr.at[3])
-    around(meta, 0, 1, ms, mr.at[3])
+    around(qall, 0, qs, qr.at[0])
+    around(meta, 0, ms, mr.at[0])
 
     sib = {"inst": me + 1 - 2 * c}
     copies = {}
@@ -193,29 +218,6 @@
                 pass_x(dz, 3, -1)
             across(dz, 1)
             across(dz, 3)
-
-    prow, plane = iota((128, 128), 0), iota((128, 128), 1)
-    perm = plane == (prow & 7) * HEADS + (prow >> 6) * GROUP + ((prow >> 3) & 7)
-    qp = dot(perm.astype(F32).astype(BF16), q).astype(BF16)
-    tokens = HOME * BT
-    spread = (iota((128, tokens), 1) >> 6) == iota((128, tokens), 0)
-    vtok = dot(home.astype(F32).astype(BF16), spread.astype(F32).astype(BF16))
-    bias = jnp.where((iota((R, tokens), 1) & (BT - 1)).astype(F32) < vtok, 0.0, LOW)
-    loads[0].wait()
-    loads[1].wait()
-    short = iota((R, 1), 0).astype(F32) != longest
-    outs = []
-    for k in range(KV):
-        keys = kbuf[pl.ds(0, HOME), k].reshape(tokens, HD)
-        values = vbuf[pl.ds(0, HOME), k].reshape(tokens, HD)
-        s = dot_t(qp[k * 64 : (k + 1) * 64], keys).reshape(GROUP, R, tokens) * SCALE + bias[None]
-        top = jnp.max(s, axis=-1, keepdims=True)
-        p = jnp.exp2(s - top)
-        total = jnp.sum(p, axis=-1, keepdims=True)
-        o = dot(p.reshape(64, tokens).astype(BF16), values).reshape(GROUP, R, HD)
-        outs.append(jnp.where(short[None], o / total, 0.0))
-    for g in range(GROUP):
-        abuf[me, :, g * HD : (g + 1) * HD] = jnp.concatenate([outs[0][g], outs[1][g]], axis=0).astype(BF16)
 
     pass_z(0, 1)
     pass_z(0, -1)
@@ -254,51 +256,46 @@
         return jnp.where(i < 5, (step * (1 - 2 * ((i + 1) % 2))) & (ZN - 1), jnp.where(i == 5, 4, jnp.where(i == 6, 3, 5)))
 
     def send_r(i, zh):
-        for dx, dc in AROUND:
+        def one(dx, dc):
             e = ((x + dx) & 3) * 2 + (c ^ dc)
             to = {"inst": zh * 8 + e}
             remote(ssend.at[i, e], srecv.at[i, xc], ss, sr.at[i], to).start()
             remote(rsend.at[i, e], rrecv.at[i, xc], rs, rr.at[i], to).start()
 
+        for dx, dc in AROUND[:-1]:
+            one(dx, dc)
+
+        @pl.when(i > 0)
+        def _():
+            one(0, 0)
+
     def lend_z(i, carry):
         zh = (z - near(i)) & 7
+        drain(qall.at[0, pl.ds(0, 7)], qr.at[i])
+        drain(meta.at[0, pl.ds(0, 7)], mr.at[i])
         lend(i, zh)
         send_r(i, zh)
         return carry
 
-    def wait_q(batch):
-        first, count = BATCHES[batch]
-        drain(qall.at[pl.ds(0, count), pl.ds(0, 7)], qr.at[batch])
-        drain(meta.at[pl.ds(0, count), pl.ds(0, 7)], mr.at[batch])
-
-    relay_q(0)
-    relay_q(1)
+    lax.fori_loop(1, 5, relay_q, 0)
     take("z", 1)
     pass_z(1, 1)
     take("z", 7)
     pass_z(7, -1)
-    drain(qall.at[0, pl.ds(0, 7)], qr.at[3])
-    drain(meta.at[0, pl.ds(0, 7)], mr.at[3])
-    lend(0, z)
-    for dx, dc in AROUND[:-1]:
-        e = ((x + dx) & 3) * 2 + (c ^ dc)
-        remote(ssend.at[0, e], srecv.at[0, xc], ss, sr.at[0], {"inst": z * 8 + e}).start()
-        remote(rsend.at[0, e], rrecv.at[0, xc], rs, rr.at[0], {"inst": z * 8 + e}).start()
-    srecv[0, xc] = ssend[0, xc]
-    rrecv[0, xc] = rsend[0, xc]
-    relay_q(2)
+    lax.fori_loop(0, 1, lend_z, 0)
+    lax.fori_loop(5, 8, relay_q, 0)
     start_x(0, 1, 7)
     take("z", 2)
     pass_z(2, 1)
     take("z", 6)
     pass_z(6, -1)
-    for batch, (first, count) in enumerate(BATCHES):
-        wait_q(batch)
-        lax.fori_loop(first, first + count, lend_z, 0)
-        if batch == 0:
-            take("z", 3)
-            pass_z(3, 1)
-            start_x(2, 6)
+    lax.fori_loop(1, 3, lend_z, 0)
+    take("z", 3)
+    pass_z(3, 1)
+    start_x(2, 6)
+    lax.fori_loop(3, 8, lend_z, 0)
+    srecv[0, xc] = ssend[0, xc]
+    rrecv[0, xc] = rsend[0, xc]
     take("z", 5)
     start_x(3, 5)
     take("z", 4)
@@ -356,10 +353,9 @@
         mine = lane8 == 2 * (zh * 8 + row8)
         owner = jnp.sum(jnp.where(mine, meta[i].reshape(8, 128), 0).astype(F32), axis=-1, keepdims=True)
         own[zh] = jnp.broadcast_to(owner, (8, 128))
-    drain(a2.at[0, pl.ds(0, 7)], gr.at[0])
-    for i in range(1, 8):
-        drain(a2.at[i], gr.at[i])
-    a2f[...] = a2[...].astype(F32).reshape(N_INST * HEADS, HD)
+    for i in (0, 1, 2, 3, 4, 6, 7, 5):
+        drain(a2.at[i] if i else a2.at[0, pl.ds(0, 7)], gr.at[i])
+        a2f[i * 128 : i * 128 + 128] = a2[i].astype(F32).reshape(128, HD)
     left = [a2f[pl.ds(h, N_INST, stride=HEADS), :].astype(BF16) for h in range(HEADS)]
     t2 = dot(jnp.concatenate(left[:8], axis=1), wbuf[0]) + dot(jnp.concatenate(left[8:], axis=1), wbuf[1])
     for i in range(8):
@@ -368,19 +364,18 @@
         to = (tp + d) % TP
         ycopies.append(remote(y2send.at[pl.ds(2 * to, 2)], y2recv.at[d], y2s.at[d], y2r.at[d], {"tp": to}))
         ycopies[-1].start()
+    for copy in list(copies.values()):
+        copy.wait_send()
+    for ref, sem in ((qall, qs), (meta, ms), (rsend, rs), (ssend, ss), (a2, gs)):
+        drain(ref.at[pl.ds(0, 7)], sem)
+        drain(ref.at[0, pl.ds(0, 7)], sem)
     for copy in ycopies:
-        copy.wait_recv()
+        copy.wait()
     long = (y2send[pl.ds(2 * tp, 2)] + y2recv[1] + y2recv[2] + y2recv[3]).reshape(16, 128)
     frow = row8.astype(F32)
     owner = own[pl.ds(2 * tp, 2)].reshape(16, 128)
     added = [jnp.where(frow == owner[i : i + 1], long[i : i + 1], 0.0) for i in range(N_INST // TP)]
     out_ref[...] = (ysend[tp] + yrecv[1] + yrecv[2] + yrecv[3] + jnp.concatenate(added, axis=0)).astype(BF16)
-
-    for copy in ycopies + list(copies.values()):
-        copy.wait_send()
-    for ref, sem in ((qall, qs), (meta, ms), (rsend, rs), (ssend, ss), (a2, gs)):
-        drain(ref.at[pl.ds(0, 7)], sem)
-        drain(ref.at[0, pl.ds(0, 7)], sem)
 
 
 def local(queries, keys_cache, value_block_cache, block_table, ctx_len, out_weight):
@@ -396,6 +391,8 @@
             pltpu.VMEM((R * HEADS, HD), BF16),
             pltpu.VMEM((R, MAXB), jnp.int32),
             pltpu.SMEM((R,), jnp.int32),
+            pltpu.VMEM((R * HEADS, HD), BF16),
+            pltpu.VMEM((KV, GROUP, R, HD), F32),
             pltpu.VMEM((PAGES, KV, BT, HD), BF16),
             pltpu.VMEM((PAGES, KV, BT, HD), BF16),
             pltpu.VMEM((2, HEADS * HD // 2, HD), BF16),
@@ -414,7 +411,7 @@
             pltpu.VMEM((8, 8, HD), F32),
             pltpu.VMEM((TP, 2, 8, HD), F32),
             dma((9,)),
-            dma, dma, dma((4,)), dma((4,)), dma((ZN,)), dma((ZN,)),
+            dma, dma, dma((ZN,)), dma((ZN,)), dma((ZN,)), dma((ZN,)),
             dma((ZN,)), dma((ZN,)),
             dma((4 * ZN,)), dma((4 * ZN,)),
             dma((4 * ZN,)), dma((4 * ZN,)),

time: 44.3 us -> 43.9 us (level)
  no operation moved by 1% of the time
where the time goes in v4:
time: 43.9 us; the launch traced here: 43.8 us
  Pallas kernels  43.2 us (98%)
  local copies, waits for them, and re-layouts  0.62 us (1%)
    pallas_call x1, Pallas kernels, local(): pl.pallas_call(kernel, out_shape=pltpu.VMEM((N_INST * R // TP, HD), BF16)...  43.2 us

profile of v4, /device:TPU:1, one launch (start us, length us, event | category | flops | bytes accessed | tf_op | source)
XLA Modules:
  0.0 43.8 jit_solution(8286462168520191769)
XLA Ops:
  0.0 43.2 %paged_decode.1 = bf16[128,128]{1,0:T(8,128)(2,1)S(1)} custom-call(bf16[128,128]{1,0:T(8,128)(2,1)} %bitcast.1, bf16[154,2,64,128]{3,2,1,0:T(8,128)(2,1)} %k_hbm.1, bf16[154,2,64,128]{3,2,1,0:T(8,128)(2,1)} %v_hbm.1, s32[8,48]{1,0:T(8,128)} %tab_hbm.1, s32[8]{0:T(128)} %ctx_hbm.1, bf16[2048,128]{1,0:T(8,128)(2,1)} %w_hbm.1), custom_call_target="tpu_custom_call" | custom-call | tf_op jit(solution)/shard_map/paged_decode/pallas_call | solution.py:385
  43.2 0.6 %copy.8 = bf16[128,128]{1,0:T(8,128)(2,1)} copy(bf16[128,128]{1,0:T(8,128)(2,1)S(1)} %paged_decode.1) | data formatting | bytes 65536

commit v5 on v4

--- a/solution.py
+++ b/solution.py
@@ -160,7 +160,7 @@
 
     def around(ref, i, send, recv):
         block = ref.at[i, xc]
-        for e in range(1, 8):
+        for e in (4, 5, 3, 2, 6, 7, 1):
             remote(block, block, send, recv, {"inst": z * 8 + ((xc + e) & 7)}).start()
 
     def relay_q(i, carry):

time: 43.9 us -> 43.5 us (level)
  no operation moved by 1% of the time
where the time goes in v5:
time: 43.5 us
  Pallas kernels  42.8 us (98%)
  local copies, waits for them, and re-layouts  0.62 us (1%)
    pallas_call x1, Pallas kernels, local(): pl.pallas_call(kernel, out_shape=pltpu.VMEM((N_INST * R // TP, HD), BF16)...  42.8 us

profile of v5, /device:TPU:1, one launch (start us, length us, event | category | flops | bytes accessed | tf_op | source)
XLA Modules:
  0.0 43.5 jit_solution(3180028768163089332)
XLA Ops:
  0.0 42.8 %paged_decode.1 = bf16[128,128]{1,0:T(8,128)(2,1)S(1)} custom-call(bf16[128,128]{1,0:T(8,128)(2,1)} %bitcast.1, bf16[154,2,64,128]{3,2,1,0:T(8,128)(2,1)} %k_hbm.1, bf16[154,2,64,128]{3,2,1,0:T(8,128)(2,1)} %v_hbm.1, s32[8,48]{1,0:T(8,128)} %tab_hbm.1, s32[8]{0:T(128)} %ctx_hbm.1, bf16[2048,128]{1,0:T(8,128)(2,1)} %w_hbm.1), custom_call_target="tpu_custom_call" | custom-call | tf_op jit(solution)/shard_map/paged_decode/pallas_call | solution.py:385
  42.8 0.6 %copy.8 = bf16[128,128]{1,0:T(8,128)(2,1)} copy(bf16[128,128]{1,0:T(8,128)(2,1)S(1)} %paged_decode.1) | data formatting | bytes 65536
